TPU v7x, 32 devices: a whole 2x2x4 slice. The times are simulated.
32 devices in a mesh: particle: 4 (over z), slab: 4 (over y, x), half: 2 (over core).
Axes of the slice: x: 2, y: 2, z: 4, core: 2. Of those that a mesh axis runs over, the one named last changes fastest.
Arguments:
- tiles: bfloat16 [2, 256, 16, 4096], P('half', 'particle', 'slab'), may hold values from -1.5 to 1.5
- tile_index: int32 [2, 256, 16], P('half', 'particle', 'slab'), may hold values from 0 to 2047
- pose_bin: int32 [2, 256], P('half', 'particle'), may hold values from 0 to 31
- bin_gain: bfloat16 [2, 32], P('half'), may hold values from 0.25 to 4
- cutoffs: int32 [6], replicated, may hold values from 32 to 128, as said below
Outputs:
- refined: float32 [2, 256, 256, 256], P('half', None, ('particle', 'slab'))
Inputs may be any that keep to these rules, and one draw needn't show every extreme that they name: `cutoffs`: the last band's cutoff is 128.
All inputs are finite; a program needn't handle non-finite values.
Results may differ from a plain program's by a relative error of at most 0.0003.
Values sent between devices are 32-bit elements; how exact they have to be, the bound alone decides.
A program may use at most 256 MiB of HBM per device.

v0:
```python
import math

import jax
import jax.numpy as jnp
from jax import lax
from jax.sharding import PartitionSpec as P

BOX = 256
TILE_ROWS = 8


error_floor = 1.0
highest = lax.Precision.HIGHEST


def from_partner(array, axis, bit):
    return lax.ppermute(array, axis, [(i, i ^ 1 << bit) for i in range(lax.axis_size(axis))])


def with_halo(cells, sides, width):
    for axis, dim in sides:
        count = lax.axis_size(axis)
        head = lax.slice_in_dim(cells, 0, width, axis=dim)
        tail = lax.slice_in_dim(cells, cells.shape[dim] - width, cells.shape[dim], axis=dim)
        cells = jnp.concatenate(
            [
                lax.ppermute(tail, axis, [(i, (i + 1) % count) for i in range(count)]),
                cells,
                lax.ppermute(head, axis, [((i + 1) % count, i) for i in range(count)]),
            ],
            axis=dim,
        )
    return cells


def signed_wave(frequency, length):
    return (frequency + length // 2) % length - length // 2


def wave_tables(frequency, places, length):
    phase_step = frequency[..., None] * places % length
    angles = phase_step.astype(jnp.float32) * (2.0 * math.pi / length)
    return (jnp.cos(angles), jnp.sin(angles))


def on_device(tiles, tile_index, pose_bin, bin_gain, cutoffs):
    slab_count = lax.axis_size("slab")
    group_count = lax.axis_size("particle")
    slab_pos = lax.axis_index("slab")
    group_pos = lax.axis_index("particle")
    half_pos = lax.axis_index("half")
    slab_depth = BOX // slab_count
    planes = slab_depth // group_count
    blocks = BOX // TILE_ROWS
    slot_count = slab_depth * blocks
    tile_width = 2 * TILE_ROWS * BOX
    touched = tile_index.shape[2]
    flat_tiles = tiles[0].reshape(-1, tile_width)
    entry_slot = tile_index[0].reshape(-1)
    bin_ids = jnp.arange(bin_gain.shape[1], dtype=jnp.int32)
    particle_gain = jnp.sum(
        jnp.where(
            pose_bin[0][:, None] == bin_ids[None, :], bin_gain[0][None, :].astype(jnp.float32), 0.0
        ),
        axis=1,
    )
    entry_gain = jnp.repeat(particle_gain, touched)
    slot_ids = jnp.arange(slot_count, dtype=jnp.int32)
    placing = jnp.where(slot_ids[:, None] == entry_slot[None, :], entry_gain[None, :], 0.0).astype(
        jnp.bfloat16
    )
    owned_slab = lax.psum_scatter(
        jnp.dot(placing, flat_tiles, preferred_element_type=jnp.float32),
        "particle",
        scatter_dimension=0,
        tiled=True,
    )
    spectrum = owned_slab.reshape(planes, blocks, 2, TILE_ROWS, BOX)
    col_freq = jnp.arange(BOX, dtype=jnp.int32)
    row_freq = col_freq.reshape(blocks, TILE_ROWS)
    plane_freq = slab_pos * slab_depth + group_pos * planes + jnp.arange(planes, dtype=jnp.int32)
    plane_sq = signed_wave(plane_freq, BOX) ** 2
    row_sq = signed_wave(row_freq, BOX) ** 2
    col_sq = signed_wave(col_freq, BOX) ** 2
    radius = plane_sq[:, None, None, None] + row_sq[None, :, :, None] + col_sq[None, None, None, :]
    inside = radius[None] <= (cutoffs * cutoffs)[:, None, None, None, None]
    masked = jnp.where(inside[:, :, :, None], spectrum[None], 0.0)
    cosine_cols, sine_cols = wave_tables(col_freq, col_freq, BOX)
    times_cos = jnp.einsum("bpwcrk,kx->bpwcrx", masked, cosine_cols, precision=highest)
    times_sin = jnp.einsum("bpwcrk,kx->bpwcrx", masked, sine_cols, precision=highest)
    part_real = times_cos[:, :, :, 0] - times_sin[:, :, :, 1]
    part_imag = times_sin[:, :, :, 0] + times_cos[:, :, :, 1]
    stacked = jnp.stack([part_real, part_imag], axis=2)
    cosine_rows, sine_rows = wave_tables(row_freq, col_freq, BOX)
    summed_cos = jnp.einsum("bpcwrx,wry->bpcyx", stacked, cosine_rows, precision=highest)
    summed_sin = jnp.einsum("bpcwrx,wry->bpcyx", stacked, sine_rows, precision=highest)
    mixed = jnp.stack(
        [summed_cos[:, :, 0] - summed_sin[:, :, 1], summed_sin[:, :, 0] + summed_cos[:, :, 1]],
        axis=2,
    )
    gathered = lax.all_to_all(mixed, ("particle", "slab"), split_axis=3, concat_axis=1, tiled=True)
    positions = jnp.arange(BOX, dtype=jnp.int32)
    source = positions // planes
    plane_order = (
        source % slab_count * slab_depth + source // slab_count * planes + positions % planes
    )
    cosine_planes, sine_planes = wave_tables(plane_order, col_freq, BOX)
    filtered = jnp.einsum("bqyx,qz->bzyx", gathered[:, :, 0], cosine_planes, precision=highest)
    filtered = filtered - jnp.einsum(
        "bqyx,qz->bzyx", gathered[:, :, 1], sine_planes, precision=highest
    )
    filtered = filtered / BOX
    subset = filtered.shape[0] // 2
    own_part = lax.dynamic_slice_in_dim(filtered, half_pos * subset, subset, 0)
    outgoing = lax.dynamic_slice_in_dim(filtered, (1 - half_pos) * subset, subset, 0)
    partner = from_partner(outgoing, "half", 0)
    squared = (own_part - partner) ** 2
    padded = with_halo(squared, ((("particle", "slab"), 2),), 1)
    rows_here = squared.shape[2]
    smoothed = (
        padded[:, :, 0:rows_here]
        + padded[:, :, 1 : rows_here + 1]
        + padded[:, :, 2 : rows_here + 2]
    )
    smoothed = smoothed + jnp.roll(smoothed, 1, axis=1) + jnp.roll(smoothed, -1, axis=1)
    smoothed = smoothed + jnp.roll(smoothed, 1, axis=3) + jnp.roll(smoothed, -1, axis=3)
    errors = smoothed / 27.0
    other_errors = from_partner(errors, "half", 0)
    errors = jnp.where(
        half_pos == 0,
        jnp.concatenate([errors, other_errors], axis=0),
        jnp.concatenate([other_errors, errors], axis=0),
    )
    weights = 1.0 / (errors + error_floor)
    blended = jnp.sum(weights * filtered, axis=0) / jnp.sum(weights, axis=0)
    return blended[None]


def solution(mesh):
    placed = (
        P("half", "particle", "slab", None),
        P("half", "particle", "slab"),
        P("half", "particle"),
        P("half", None),
        P(),
    )
    return jax.shard_map(
        on_device,
        mesh=mesh,
        in_specs=placed,
        out_specs=P("half", None, ("particle", "slab"), None),
        check_vma=False,
    )
```

profile of v0, /device:TPU:25, one launch (start us, length us, event | category | flops | bytes accessed | tf_op | source)
XLA Modules:
  0.0 2565.6 jit_solution(3926110211337472506)
XLA Ops:
  6.5 2.5 reshape_squeeze.3
  9.1 0.8 copy.35
  10.0 0.7 bitcast_convert_fusion
  10.6 0.7 select_reduce_fusion
  11.6 13.3 fusion.34
  25.0 0.5 copy-done.2
  25.5 1.0 fusion.140
  26.5 1.0 fusion.142
  27.5 1.0 fusion.144
  28.5 1.7 fusion.146
  30.3 0.6 broadcast_add_fusion
  30.9 6.2 broadcast_compare_fusion
  37.1 540.6 %reduce-scatter.2.cloned.1.call-done = f32[512,4096]{1,0:T(8,128)} async-done(((f32[2048,4096]{1,0:T(8,128)}), f32[512,4096]{1,0:T(8,128)}) %reduce-scatter.2.cloned.1.call-update) | async-done | bytes 8388624 | tf_op jit(solution)/shard_map/reduce_scatter | solution.py:72
  577.7 7.5 copy.57
  585.2 45.0 %fusion = f32[6,16,32,2,8,256]{5,4,3,2,1,0:T(8,128)} fusion(f32[16,32,2,8,256]{4,3,2,1,0:T(8,128)S(1)} %bitcast.102, pred[6,16,32,8,256]{4,3,2,1,0:T(8,128)(4,1)} %broadcast_compare_fusion, f32[256,256,1,1,1,1]{0,1,5,4,3,2:T(8,128)S(1)} %fusion.140), kind=kOutput, calls=%fused_computation | convolution fusion | flops 38667288576 | bytes 65273856 | tf_op jit(solution)/shard_map/bpwcrk,kx->bpwcrx/dot_general | solution.py:90
  630.2 45.3 %fusion.2 = f32[6,16,32,2,8,256]{5,4,3,2,1,0:T(8,128)} fusion(f32[16,32,2,8,256]{4,3,2,1,0:T(8,128)S(1)} %bitcast.103, pred[6,16,32,8,256]{4,3,2,1,0:T(8,128)(4,1)} %broadcast_compare_fusion, f32[256,256,1,1,1,1]{0,1,5,4,3,2:T(8,128)S(1)} %fusion.142), kind=kOutput, calls=%fused_computation.2 | convolution fusion | flops 38667288576 | bytes 65273856 | tf_op jit(solution)/shard_map/bpwcrk,kx->bpwcrx/dot_general | solution.py:89
  675.5 25.6 fusion.12
  701.2 25.8 %fusion.10 = f32[6,16,1,32,8,256]{5,4,3,1,0,2:T(8,128)} fusion(f32[6,16,32,2,8,256]{5,4,3,2,1,0:T(8,128)} %fusion.2, f32[6,16,32,2,8,256]{5,4,3,2,1,0:T(8,128)} %fusion), kind=kLoop, calls=%fused_computation.17 | loop fusion | flops 6291456 | bytes 75497472 | tf_op jit(solution)/shard_map/add | solution.py:92
  727.0 34.1 %pad_maximum_fusion = f32[6,16,2,32,8,256]{5,4,3,1,0,2:T(8,128)} fusion(f32[6,16,1,32,8,256]{5,4,3,1,0,2:T(8,128)} %fusion.10, f32[6,16,1,32,8,256]{5,4,3,1,0,2:T(8,128)} %fusion.12), kind=kLoop, calls=%fused_computation.4 | loop fusion | flops 12582912 | bytes 100663296 | tf_op jit(solution)/shard_map/stack | solution.py:93
  761.1 64.0 %fusion.22 = f32[6,16,2,256,256]{4,3,2,1,0:T(8,128)} fusion(f32[6,16,2,32,8,256]{5,4,3,1,0,2:T(8,128)} %pad_maximum_fusion, f32[32,8,256,1,1,1]{2,0,1,5,4,3:T(8,128)S(1)} %fusion.144), kind=kOutput, calls=%fused_computation.34 | convolution fusion | flops 38654705664 | bytes 100925440 | tf_op jit(solution)/shard_map/bpcwrx,wry->bpcyx/dot_general | solution.py:95
  825.1 63.9 %fusion.25 = f32[6,16,2,256,256]{4,3,2,1,0:T(8,128)} fusion(f32[6,16,2,32,8,256]{5,4,3,1,0,2:T(8,128)} %pad_maximum_fusion, f32[32,8,256,1,1,1]{2,0,1,5,4,3:T(8,128)S(1)} %copy-done.1), kind=kOutput, calls=%fused_computation.35 | convolution fusion | flops 38654705664 | bytes 100925440 | tf_op jit(solution)/shard_map/bpcwrx,wry->bpcyx/dot_general | solution.py:96
  889.0 49.2 %slice_subtract_fusion = (f32[6,16,1,256,256]{4,3,2,1,0:T(8,128)}, f32[6,16,1,256,256]{4,3,2,1,0:T(8,128)}) fusion(f32[6,16,2,256,256]{4,3,2,1,0:T(8,128)} %fusion.25, f32[6,16,2,256,256]{4,3,2,1,0:T(8,128)} %fusion.22), kind=kLoop, calls=%fused_computation.15 | loop fusion | flops 12582912 | bytes 150994944 | tf_op jit(solution)/shard_map/sub | solution.py:98
  938.2 34.3 %pad_maximum_fusion.1 = f32[6,16,2,256,256]{4,3,2,1,0:T(8,128)} fusion(f32[6,16,1,256,256]{4,3,2,1,0:T(8,128)} %get-tuple-element.8, f32[6,16,1,256,256]{4,3,2,1,0:T(8,128)} %get-tuple-element.7), kind=kLoop, calls=%fused_computation.5 | loop fusion | flops 12582912 | bytes 100663296 | tf_op jit(solution)/shard_map/stack | solution.py:97
  972.5 82.1 %copy.42 = f32[6,16,2,256,256]{4,2,1,0,3:T(2,128)} copy(f32[6,16,2,256,256]{4,3,2,1,0:T(8,128)} %pad_maximum_fusion.1) | data formatting | bytes 100663296 | tf_op jit(solution)/shard_map/stack | solution.py:97
  1054.6 6.8 all-to-all-start
  1061.4 1091.9 %all-to-all-done = f32[6,16,2,256,256]{4,2,1,0,3:T(2,128)} async-done(((f32[6,16,2,256,256]{4,2,1,0,3:T(2,128)}), f32[6,16,2,256,256]{4,2,1,0,3:T(2,128)}, u32[]{:S(2)}, u32[]{:S(2)}) %all-to-all-start) | async-done | bytes 50331680 | tf_op jit(solution)/shard_map/all_to_all | solution.py:101
  2153.4 37.6 %copy.43 = f32[6,16,2,16,16,256]{5,1,3,4,0,2:T(8,128)} copy(f32[6,16,2,16,16,256]{5,2,1,0,4,3:T(2,128)} %bitcast.20) | data formatting | bytes 100663296 | tf_op jit(solution)/shard_map/all_to_all | solution.py:101
  2191.0 32.2 %fusion.8 = f32[256,6,16,256]{3,0,2,1:T(8,128)} fusion(f32[6,256,2,16,256]{4,1,3,0,2:T(8,128)} %bitcast.104, s32[256]{0:T(256)S(1)} %fusion.79), kind=kOutput, calls=%fused_computation.11 | convolution fusion | flops 19328270336 | bytes 50332672 | tf_op jit(solution)/shard_map/bqyx,qz->bzyx/dot_general | solution.py:109
  2223.2 36.0 %subtract_multiply_fusion = f32[256,6,16,256]{3,0,2,1:T(8,128)} fusion(f32[256,6,16,256]{3,0,2,1:T(8,128)} %fusion.8, f32[6,256,2,16,256]{4,1,3,0,2:T(8,128)} %bitcast.105, s32[256]{0:T(256)S(1)} %fusion.79), kind=kOutput, calls=%fused_computation.27 | convolution fusion | flops 19340853248 | bytes 75498496 | tf_op jit(solution)/shard_map/bqyx,qz->bzyx/dot_general | solution.py:108
  2259.2 10.6 dynamic-slice_bitcast_fusion
  2269.8 3.1 collective-permute-start
  2272.9 19.1 collective-permute-done
  2292.0 9.0 fusion.33
  2301.3 42.0 %collective-permute-start.2 = (f32[3,256,1,256]{3,1,2,0:T(8,128)S(1)}, f32[3,256,1,256]{3,1,2,0:T(8,128)S(1)}, u32[]{:S(2)}, u32[]{:S(2)}) collective-permute-start(f32[3,256,1,256]{3,1,2,0:T(8,128)S(1)} %get-tuple-element.18), channel_id=1, source_target_pairs={{2,0},{4,2},{6,4},{8,6},{10,8},{12,10},{14,12},{16,14},{18,16},{20... | collective-permute-start | bytes 2359304 | tf_op jit(solution)/shard_map/ppermute | solution.py:29
  2343.4 17.5 collective-permute-done.1
  2360.9 43.0 %collective-permute-done.2 = f32[3,256,1,256]{3,1,2,0:T(8,128)S(1)} collective-permute-done((f32[3,256,1,256]{3,1,2,0:T(8,128)S(1)}, f32[3,256,1,256]{3,1,2,0:T(8,128)S(1)}, u32[]{:S(2)}, u32[]{:S(2)}) %collective-permute-start.2) | collective-permute-done | bytes 786464 | tf_op jit(solution)/shard_map/ppermute | solution.py:29
  2403.9 6.0 fusion.28
  2409.9 19.9 fusion.118
  2429.8 1.2 fusion.119
  2431.0 24.5 fusion.30
  2455.5 21.1 fusion.116
  2476.6 9.3 fusion.117
  2486.0 21.0 fusion.32
  2507.0 1.2 collective-permute-start.3
  2508.2 19.1 collective-permute-done.3
  2527.3 25.9 %fusion.115 = (f32[256,16,256]{2,0,1:T(8,128)S(1)}, f32[256,16,256]{2,0,1:T(8,128)S(1)}) fusion(f32[3,256,16,256]{3,1,2,0:T(8,128)} %fusion.32, f32[3,256,16,256]{3,1,2,0:T(8,128)} %collective-permute-done.3, pred[]{:T(512)S(6)} %eq.46, f32[256,6,16,256]{3,0,2,1:T(8,128)} %subtract_multiply_fusion), kind=kLoop, calls=%fused_computation.161 | loop fusion | flops 48234496 | bytes 58720256 | tf_op jit(solution)/shard_map/reduce_sum | solution.py:135
  2553.3 0.8 divide_bitcast_fusion
  2554.1 4.4 copy.44
  (20 shorter events, 0.8 us)
Async XLA Ops:
  6.5 571.2 %reduce-scatter.2.cloned.1.call-start = ((), (), s32[]{:S(2)}) async-start(), calls=%async_computation.2 | async-start | bytes 41943040 | tf_op jit(solution)/shard_map/reduce_scatter | solution.py:72
  24.8 0.7 copy-start.2
  761.1 64.0 %copy-start.1 = (f32[32,8,256,1,1,1]{2,0,1,5,4,3:T(8,128)S(1)}, f32[32,8,256,1,1,1]{2,0,1,5,4,3:T(8,128)}, u32[]{:S(2)}) copy-start(f32[32,8,256,1,1,1]{2,0,1,5,4,3:T(8,128)} %fusion.146) | copy-start | bytes 786436
  1054.6 1098.7 %all-to-all-start = ((f32[6,16,2,256,256]{4,2,1,0,3:T(2,128)}), f32[6,16,2,256,256]{4,2,1,0,3:T(2,128)}, u32[]{:S(2)}, u32[]{:S(2)}) async-start(f32[6,16,2,256,256]{4,2,1,0,3:T(2,128)} %copy.42), calls=%async_computation.1 | async-start | bytes 100663296 | tf_op jit(solution)/shard_map/all_to_all | solution.py:101
  2269.8 22.2 collective-permute-start
  2301.1 108.8 %copy-start = (f32[3,256,16,256]{3,1,2,0:T(8,128)}, f32[3,256,16,256]{3,1,2,0:T(8,128)S(1)}, u32[]{:S(2)}) copy-start(f32[3,256,16,256]{3,1,2,0:T(8,128)S(1)} %fusion.33) | copy-start | bytes 37748740
  2301.3 59.6 %collective-permute-start.1 = (f32[3,256,1,256]{3,1,2,0:T(8,128)S(1)}, f32[3,256,1,256]{3,1,2,0:T(8,128)S(1)}, u32[]{:S(2)}, u32[]{:S(2)}) collective-permute-start(f32[3,256,1,256]{3,1,2,0:T(8,128)S(1)} %get-tuple-element.17), channel_id=1, source_target_pairs={{0,2},{2,4},{4,6},{6,8},{8,10},{10,12},{12,14},{14,16},{16,18},{18... | collective-permute-start | bytes 2359304 | tf_op jit(solution)/shard_map/ppermute | solution.py:27
  2301.3 102.6 %collective-permute-start.2 = (f32[3,256,1,256]{3,1,2,0:T(8,128)S(1)}, f32[3,256,1,256]{3,1,2,0:T(8,128)S(1)}, u32[]{:S(2)}, u32[]{:S(2)}) collective-permute-start(f32[3,256,1,256]{3,1,2,0:T(8,128)S(1)} %get-tuple-element.18), channel_id=1, source_target_pairs={{2,0},{4,2},{6,4},{8,6},{10,8},{12,10},{14,12},{16,14},{18,16},{20... | collective-permute-start | bytes 2359304 | tf_op jit(solution)/shard_map/ppermute | solution.py:29
  2507.0 20.3 collective-permute-start.3
Sparse Core Ops, SparseCore 0:
  25.0 552.7 reduce-scatter.1
where the time goes:
time: 2570 us
  waiting for transfers between devices  1730 us (67%)
  matrix products  300 us (12%)
  other arithmetic  269 us (10%)
  local copies, waits for them, and re-layouts  198 us (8%)
  starting transfers between devices  53.2 us (2%)
    all_to_all x1, waiting for transfers between devices, on_device(): lax.all_to_all(mixed, ('particle', 'slab'), split_axis=3, concat_axis=1,...  1090 us
    reduce_scatter x1, waiting for transfers between devices, on_device(): lax.psum_scatter(jnp.dot(placing, flat_tiles, preferred_element_type=jnp....  541 us
    another operation x1, local copies, waits for them, and re-layouts, on_device(): jnp.stack([summed_cos[:, :, 0] - summed_sin[:, :, 1], summed_sin[:, :, 0]...  82.1 us
    dot_general x1, matrix products, on_device(): jnp.einsum('bpcwrx,wry->bpcyx', stacked, cosine_rows, precision=highest)  64 us
    dot_general x1, matrix products, on_device(): jnp.einsum('bpcwrx,wry->bpcyx', stacked, sine_rows, precision=highest)  63.9 us
  transfers between devices with their start and end apart: 6, of which 6 were waited for; matrix products, arithmetic and copies ran while one was open for 0% of the time, Pallas kernels for 0%

commit v1 on v0

v1 whole, which is shorter than its diff:
```python
import functools
import math

import jax
import jax.numpy as jnp
from jax import lax
from jax.experimental import pallas as pl
from jax.experimental.pallas import tpu as pltpu
from jax.sharding import PartitionSpec as P

BOX = 256
TILE_ROWS = 8
CHUNK_BANDS = 2

error_floor = 1.0
high = lax.Precision.HIGH


def from_partner(array, axis, bit):
    return lax.ppermute(array, axis, [(i, i ^ 1 << bit) for i in range(lax.axis_size(axis))])


def signed_wave(frequency, length):
    return (frequency + length // 2) % length - length // 2


def turn_table(frequency, places, length):
    phase_step = frequency[..., None] * places % length
    angles = phase_step.astype(jnp.float32) * (2.0 * math.pi / length)
    cosine, sine = jnp.cos(angles), jnp.sin(angles)
    from_real = jnp.stack([cosine, sine], axis=-2)
    from_imag = jnp.stack([-sine, cosine], axis=-2)
    return jnp.stack([from_real, from_imag], axis=-3)


def blend_kernel(first, last, step_planes, *refs):
    if first:
        own_ref, other_ref, low_ref, high_ref, *outs = refs
        num_in = den_in = None
    else:
        own_ref, other_ref, low_ref, high_ref, num_in, den_in, *outs = refs
    if last:
        out_ref, padded, smooth, num_ref, den_ref = outs
    else:
        num_ref, den_ref, padded, smooth = outs
    band = pl.program_id(0)
    depth, rows, width = own_ref.shape[1:]

    @pl.when(band == 0)
    def _():
        if first:
            num_ref[...] = jnp.zeros_like(num_ref)
            den_ref[...] = jnp.zeros_like(den_ref)
        else:
            num_ref[...] = num_in[...]
            den_ref[...] = den_in[...]

    def smooth_rows(step, carry):
        here = pl.ds(step * step_planes, step_planes)
        gap = own_ref[0, here] - other_ref[0, here]
        padded[:, 0:1, :] = low_ref[0, here]
        padded[:, 1 : rows + 1, :] = gap * gap
        padded[:, rows + 1 : rows + 2, :] = high_ref[0, here]
        total = (
            padded[:, 0:rows, :] + padded[:, 1 : rows + 1, :] + padded[:, 2 : rows + 2, :]
        )
        total = total + pltpu.roll(total, 1, 2) + pltpu.roll(total, width - 1, 2)
        smooth[pl.ds(step * step_planes + 1, step_planes)] = total
        return carry

    lax.fori_loop(0, depth // step_planes, smooth_rows, 0)
    smooth[0:1] = smooth[depth : depth + 1]
    smooth[depth + 1 : depth + 2] = smooth[1:2]

    def add_band(step, carry):
        start = step * step_planes
        here = pl.ds(start, step_planes)
        total = (
            smooth[here]
            + smooth[pl.ds(start + 1, step_planes)]
            + smooth[pl.ds(start + 2, step_planes)]
        )
        weight = 1.0 / (total * (1.0 / 27.0) + error_floor)
        num_ref[here] += weight * own_ref[0, here]
        den_ref[here] += weight
        return carry

    lax.fori_loop(0, depth // step_planes, add_band, 0)

    if last:

        @pl.when(band == pl.num_programs(0) - 1)
        def _():
            def divide(step, carry):
                here = pl.ds(step * step_planes, step_planes)
                out_ref[here] = num_ref[here] / den_ref[here]
                return carry

            lax.fori_loop(0, depth // step_planes, divide, 0)


def blend(own, other, low, high_rows, sums, last):
    bands, depth, rows, width = own.shape
    first = sums is None
    step_planes = 8
    map_spec = pl.BlockSpec((1, depth, rows, width), lambda b: (b, 0, 0, 0))
    row_spec = pl.BlockSpec((1, depth, 1, width), lambda b: (b, 0, 0, 0))
    whole = pl.BlockSpec((depth, rows, width), lambda b: (0, 0, 0))
    kept = jax.ShapeDtypeStruct((depth, rows, width), jnp.float32)
    scratch = [
        pltpu.VMEM((step_planes, rows + 2, width), jnp.float32),
        pltpu.VMEM((depth + 2, rows, width), jnp.float32),
    ]
    if last:
        scratch += [pltpu.VMEM((depth, rows, width), jnp.float32)] * 2
    cells = bands * depth * rows * width
    return pl.pallas_call(
        functools.partial(blend_kernel, first, last, step_planes),
        grid=(bands,),
        in_specs=[map_spec, map_spec, row_spec, row_spec] + ([] if first else [whole, whole]),
        out_specs=whole if last else [whole, whole],
        out_shape=kept if last else [kept, kept],
        scratch_shapes=scratch,
        compiler_params=pltpu.CompilerParams(vmem_limit_bytes=60 * 1024 * 1024),
        cost_estimate=pl.CostEstimate(
            flops=20 * cells, bytes_accessed=8 * cells + 16 * cells // bands, transcendentals=0
        ),
    )(own, other, low, high_rows, *([] if first else sums))


def on_device(tiles, tile_index, pose_bin, bin_gain, cutoffs):
    slab_count = lax.axis_size("slab")
    group_count = lax.axis_size("particle")
    slab_pos = lax.axis_index("slab")
    group_pos = lax.axis_index("particle")
    slab_depth = BOX // slab_count
    planes = slab_depth + 1
    group_rows = BOX // group_count
    rows_here = group_rows // slab_count
    blocks = BOX // TILE_ROWS
    slot_count = planes * blocks
    half_box = BOX // 2
    touched = tile_index.shape[2]

    entry_slot = tile_index[0].reshape(-1)
    bin_ids = jnp.arange(bin_gain.shape[1], dtype=jnp.int32)
    particle_gain = jnp.sum(
        jnp.where(
            pose_bin[0][:, None] == bin_ids[None, :], bin_gain[0][None, :].astype(jnp.float32), 0.0
        ),
        axis=1,
    )
    entry_gain = jnp.repeat(particle_gain, touched)
    entries = entry_slot.shape[0]
    parts = tiles[0].reshape(entries, 2, TILE_ROWS, BOX).transpose(0, 2, 1, 3).astype(jnp.float32)
    lane = jnp.arange(128, dtype=jnp.int32)
    notes = jnp.where(
        lane[None, :] == 0,
        entry_slot[:, None].astype(jnp.float32),
        jnp.where(lane[None, :] == 1, entry_gain[:, None], 0.0),
    )

    direct = parts[..., :half_box]
    upper = parts[:, :, :, half_box:]
    turn = lax.broadcasted_iota(jnp.int32, (half_box, half_box), 0)
    target = lax.broadcasted_iota(jnp.int32, (half_box, half_box), 1)
    swap = jnp.where((turn + target == half_box) & (target > 0), 1.0, 0.0).astype(jnp.bfloat16)
    mirrored = jnp.einsum(
        "ercx,xk->erck", upper.astype(jnp.bfloat16), swap, preferred_element_type=jnp.float32
    )
    mirrored = mirrored * jnp.array([1.0, -1.0], jnp.float32)[:, None]
    mirrored = jnp.concatenate([mirrored[:, :1], mirrored[:, :0:-1]], axis=1)

    lone = jnp.sum(
        jnp.where(
            (entry_slot == 0) & (slab_pos == 0), entry_gain * parts[:, 0, 0, half_box], 0.0
        )
    )
    lone = lax.psum(lone, ("particle", "slab"))

    width = 2 * TILE_ROWS * half_box
    send_direct = jnp.concatenate([direct.reshape(entries, width), notes], axis=1)
    send_mirror = jnp.concatenate([mirrored.reshape(entries, width), notes], axis=1)
    send_mirror = lax.ppermute(
        send_mirror, "slab", [(i, slab_count - 1 - i) for i in range(slab_count)]
    )
    all_direct = lax.all_gather(send_direct, "particle", axis=0, tiled=True)
    all_mirror = lax.all_gather(send_mirror, "particle", axis=0, tiled=True)
    all_direct, all_mirror = lax.optimization_barrier((all_direct, all_mirror))

    slot_ids = jnp.arange(slot_count, dtype=jnp.int32)
    slot_d = all_direct[:, width].astype(jnp.int32)
    gain_d = all_direct[:, width + 1]
    slot_m = all_mirror[:, width].astype(jnp.int32)
    gain_m = all_mirror[:, width + 1]
    plane_m, block_m = slab_depth - slot_m // blocks, slot_m % blocks
    slot_m0 = plane_m * blocks + (blocks - block_m) % blocks
    slot_m1 = plane_m * blocks + (blocks - 1 - block_m)
    gains = jnp.concatenate([gain_d, gain_m])

    def placing(slots):
        return jnp.where(slot_ids[:, None] == slots[None, :], gains[None, :], 0.0).astype(
            jnp.bfloat16
        )

    values = jnp.concatenate([all_direct[:, :width], all_mirror[:, :width]], axis=0).astype(
        jnp.bfloat16
    )
    row_width = 2 * half_box
    first_rows = jnp.dot(
        placing(jnp.concatenate([slot_d, slot_m0])),
        values[:, :row_width],
        preferred_element_type=jnp.float32,
    )
    other_rows = jnp.dot(
        placing(jnp.concatenate([slot_d, slot_m1])),
        values[:, row_width:],
        preferred_element_type=jnp.float32,
    )
    spectrum = jnp.concatenate([first_rows, other_rows], axis=1).reshape(
        planes, blocks, TILE_ROWS, 2, half_box
    )

    col_freq = jnp.arange(half_box, dtype=jnp.int32)
    positions = jnp.arange(BOX, dtype=jnp.int32)
    row_freq = positions.reshape(blocks, TILE_ROWS)
    plane_freq = slab_pos * slab_depth + jnp.arange(planes, dtype=jnp.int32)
    plane_sq = signed_wave(plane_freq, BOX) ** 2
    row_sq = signed_wave(row_freq, BOX) ** 2
    radius = plane_sq[:, None, None, None] + row_sq[None, :, :, None] + col_freq**2

    row_table = turn_table(
        row_freq, group_pos * group_rows + jnp.arange(group_rows, dtype=jnp.int32), BOX
    )
    row_table = row_table.reshape(blocks, TILE_ROWS, 2, 2, slab_count, rows_here)
    every_plane = (
        jnp.arange(slab_count, dtype=jnp.int32)[:, None] * slab_depth
        + jnp.arange(planes, dtype=jnp.int32)
    )
    plane_table = turn_table(every_plane, positions, BOX)
    col_table = turn_table(col_freq, positions, BOX)[:, :, 0] / BOX
    sign = jnp.where(positions % 2 == 0, 1.0 / BOX, -1.0 / BOX)

    bands = cutoffs.shape[0]
    around = slab_count * group_count
    forward = [(i, (i + 1) % around) for i in range(around)]
    backward = [((i + 1) % around, i) for i in range(around)]
    sums = None
    for start in range(0, bands, CHUNK_BANDS):
        limit = (cutoffs * cutoffs)[start : start + CHUNK_BANDS]
        inside = radius[None] <= limit[:, None, None, None, None]
        masked = jnp.where(inside[:, :, :, :, None, :], spectrum[None], 0.0)
        rows_done = jnp.einsum("bqwrck,wrcdsy->sbdqyk", masked, row_table, precision=high)
        arrived = lax.all_to_all(rows_done, "slab", split_axis=0, concat_axis=0, tiled=True)
        planes_done = jnp.einsum("sbdqyk,sqdez->bzyek", arrived, plane_table, precision=high)
        filtered = jnp.einsum("bzyek,kex->bzyx", planes_done, col_table, precision=high)
        extra = jnp.where(limit >= half_box * half_box, lone, 0.0)
        filtered = filtered + extra[:, None, None, None] * sign
        other = from_partner(filtered, "half", 0)
        head = (filtered[:, :, :1] - other[:, :, :1]) ** 2
        tail = (filtered[:, :, -1:] - other[:, :, -1:]) ** 2
        low = lax.ppermute(tail, ("particle", "slab"), forward)
        high_rows = lax.ppermute(head, ("particle", "slab"), backward)
        sums = blend(filtered, other, low, high_rows, sums, start + CHUNK_BANDS >= bands)
    return sums[None]


def solution(mesh):
    placed = (
        P("half", "particle", "slab", None),
        P("half", "particle", "slab"),
        P("half", "particle"),
        P("half", None),
        P(),
    )
    return jax.shard_map(
        on_device,
        mesh=mesh,
        in_specs=placed,
        out_specs=P("half", None, ("particle", "slab"), None),
        check_vma=False,
    )
```

time: 2570 us -> 991 us (0.39)
  waiting for transfers between devices: 1730 us -> 465 us
  other arithmetic: 269 us -> 50.2 us
  matrix products: 300 us -> 156 us
  local copies, waits for them, and re-layouts: 198 us -> 74.4 us
  blocking collectives: 0 us -> 110 us
  Pallas kernels: 0 us -> 73.6 us
    all_to_all x1 -> x3, waiting for transfers between devices: 1090 us -> 139 us  [on_device(): lax.all_to_all(rows_done, 'slab', split_axis=0, concat_axis=0, tiled=True)]
    reduce_scatter x1 -> x0, waiting for transfers between devices: 541 us -> none  [on_device(): lax.psum_scatter(jnp.dot(placing, flat_tiles, preferred_element_type=jnp....]
    all_gather x0 -> x2, waiting for transfers between devices: none -> 249 us  [the longest x1 158 us: on_device(): all_mirror = lax.all_gather(send_mirror, 'particle', axis=0, tiled=True)]
    dot_general x7 -> x12, matrix products: 300 us -> 156 us  [the longest x3 59.6 us: on_device(): jnp.einsum('bqwrck,wrcdsy->sbdqyk', masked, row_table, precision=high)]
    psum x0 -> x1, blocking collectives: none -> 110 us  [on_device(): lone = lax.psum(lone, ('particle', 'slab'))]
    another operation x2 -> x0, local copies, waits for them, and re-layouts: 84.7 us -> none  [the longest x1 82.1 us: on_device(): jnp.stack([summed_cos[:, :, 0] - summed_sin[:, :, 1], summed_sin[:, :, 0]...]
    sub x2 -> x0, other arithmetic: 74.8 us -> none  [the longest x1 49.2 us: on_device(): summed_cos[:, :, 0] - summed_sin[:, :, 1]]
    pallas_call x0 -> x3, Pallas kernels: none -> 73.6 us  [blend(): pl.pallas_call(functools.partial(blend_kernel, first, last, step_planes),...]
  transfers between devices with their start and end apart: 6 -> 15, of which waited for: 6 -> 6; matrix products, arithmetic and copies ran while one was open for 0% -> 16% of each run, Pallas kernels for 0% -> 5%
where the time goes in v1:
time: 991 us; the launch traced here: 979 us
  waiting for transfers between devices  465 us (47%)
  matrix products  156 us (16%)
  blocking collectives  110 us (11%)
  local copies, waits for them, and re-layouts  74.4 us (8%)
  Pallas kernels  73.6 us (7%)
  other arithmetic  50.2 us (5%)
  starting transfers between devices  35.7 us (4%)
  between operations  14.4 us (1%)
    all_gather x1, waiting for transfers between devices, on_device(): all_mirror = lax.all_gather(send_mirror, 'particle', axis=0, tiled=True)  158 us
    all_to_all x3, waiting for transfers between devices, on_device(): lax.all_to_all(rows_done, 'slab', split_axis=0, concat_axis=0, tiled=True)  139 us
    psum x1, blocking collectives, on_device(): lone = lax.psum(lone, ('particle', 'slab'))  110 us
    all_gather x1, waiting for transfers between devices, on_device(): all_direct = lax.all_gather(send_direct, 'particle', axis=0, tiled=True)  91.1 us
    pallas_call x3, Pallas kernels, blend(): pl.pallas_call(functools.partial(blend_kernel, first, last, step_planes),...  73.6 us
    dot_general x3, matrix products, on_device(): jnp.einsum('bqwrck,wrcdsy->sbdqyk', masked, row_table, precision=high)  59.6 us
    ppermute x1, waiting for transfers between devices, on_device(): lax.ppermute(send_mirror, 'slab', [(i, slab_count - 1 - i) for i in range...  48.4 us
    dot_general x3, matrix products, on_device(): jnp.einsum('sbdqyk,sqdez->bzyek', arrived, plane_table, precision=high)  47.7 us
  transfers between devices with their start and end apart: 15, of which 6 were waited for; matrix products, arithmetic and copies ran while one was open for 16% of the time, Pallas kernels for 5%

profile of v1, /device:TPU:25, one launch (start us, length us, event | category | flops | bytes accessed | tf_op | source)
XLA Modules:
  0.0 979.1 jit_solution(1975930221547358321)
XLA Ops:
  6.6 3.2 convert_element_type.116
  9.8 2.8 copy_bitcast_fusion
  15.4 1.7 slice.119
  17.2 1.8 copy.57
  19.0 3.1 rev.3
  22.1 1.6 pad_maximum_fusion.5
  23.9 2.3 pad_maximum_fusion.3
  26.3 2.2 collective-permute-start
  28.5 48.4 %collective-permute-done = f32[256,2176]{0,1:T(8,128)S(1)} collective-permute-done((f32[256,2176]{0,1:T(8,128)}, f32[256,2176]{0,1:T(8,128)S(1)}, u32[]{:S(2)}, u32[]{:S(2)}) %collective-permute-start) | collective-permute-done | bytes 2228256 | tf_op jit(solution)/shard_map/ppermute | solution.py:184
  80.0 3.0 broadcast_add_fusion
  83.0 8.6 broadcast_compare_fusion
  91.6 91.1 %all-gather.3.cloned.1.call-done = f32[1024,2176]{0,1:T(8,128)} async-done(((f32[256,2176]{0,1:T(8,128)}), f32[1024,2176]{0,1:T(8,128)}) %all-gather.3.cloned.1.call-update) | async-done | bytes 8912912 | tf_op jit(solution)/shard_map/all_gather | solution.py:187
  182.7 158.0 %all-gather.5.cloned.1.call-done = f32[1024,2176]{0,1:T(8,128)} async-done(((f32[256,2176]{0,1:T(8,128)}), f32[1024,2176]{0,1:T(8,128)}) %all-gather.5.cloned.1.call-update) | async-done | bytes 8912912 | tf_op jit(solution)/shard_map/all_gather | solution.py:188
  341.6 4.0 slice.173
  346.5 4.7 slice.172
  351.2 2.5 fusion.24
  353.7 19.1 %fusion.25 = f32[2080,1792]{1,0:T(8,128)S(1)} fusion(s32[2048]{0:T(1024)S(1)} %get-tuple-element.42, bf16[2048]{0:T(1024)(128)(2,1)S(1)} %pad_maximum_fusion.7, bf16[1024,2048]{0,1:T(8,128)(2,1)} %copy-done.4, bf16[1024,2048]{0,1:T(8,128)(2,1)} %copy-done.3), kind=kOutput, calls=%fused_computation.30 | convolution fusion | flops 15290466304 | bytes 23310336 | tf_op jit(solution)/shard_map/dot_general | solution.py:215
  372.8 6.4 pad_maximum_fusion
  379.2 22.5 %broadcast_in_dim.201 = f32[65,32,8,2,128]{4,3,2,1,0:T(2,128)} reshape(f32[2080,2048]{1,0:T(8,128)} %pad_maximum_fusion) | data formatting | bytes 34078720 | tf_op jit(solution)/shard_map/jit(_where)/broadcast_in_dim | solution.py:252
  401.8 12.8 %copy.59 = f32[65,32,8,2,128]{4,1,2,3,0:T(8,128)} copy(f32[65,32,8,2,128]{4,3,2,1,0:T(2,128)} %broadcast_in_dim.201) | data formatting | bytes 34078720 | tf_op jit(solution)/shard_map/jit(_where)/broadcast_in_dim | solution.py:252
  414.6 19.9 %fusion.45 = f32[4,2,2,65,16,128]{5,4,3,1,0,2:T(8,128)S(1)} fusion(f32[65,32,8,2,128]{4,1,2,3,0:T(8,128)} %copy.59, pred[2,65,32,8,128]{4,2,3,1,0:T(8,128)(4,1)} %get-tuple-element.27, f32[32,8,1,1,4,16]{0,5,1,2,4,3:T(8,128)S(1)} %get-tuple-element.40, f32[32,8,1,1,4,16]{0,5,1,2,4,3:T(8,128)S(1)} %get-tuple-element.39, ...), kind=kOutput, calls=%fused_computation.56 | convolution fusion | flops 6551830528 | bytes 30015488 | tf_op jit(solution)/shard_map/bqwrck,wrcdsy->sbdqyk/dot_general | solution.py:253
  434.4 4.1 copy.68
  438.6 5.9 all-to-all-start.2
  444.4 19.9 %fusion.42 = f32[4,2,2,65,16,128]{5,4,3,1,0,2:T(8,128)S(1)} fusion(f32[65,32,8,2,128]{4,1,2,3,0:T(8,128)} %copy.59, pred[2,65,32,8,128]{4,2,3,1,0:T(8,128)(4,1)} %get-tuple-element.28, f32[32,8,1,1,4,16]{0,5,1,2,4,3:T(8,128)S(1)} %get-tuple-element.40, f32[32,8,1,1,4,16]{0,5,1,2,4,3:T(8,128)S(1)} %get-tuple-element.39, ...), kind=kOutput, calls=%fused_computation.55 | convolution fusion | flops 6551830528 | bytes 30015488 | tf_op jit(solution)/shard_map/bqwrck,wrcdsy->sbdqyk/dot_general | solution.py:253
  464.3 4.2 copy.65
  468.5 69.3 %all-to-all-done.2 = f32[4,2,2,65,16,128]{5,4,3,2,1,0:T(8,128)} async-done(((f32[4,2,2,65,16,128]{5,4,3,2,1,0:T(8,128)}), f32[4,2,2,65,16,128]{5,4,3,2,1,0:T(8,128)}, u32[]{:S(2)}, u32[]{:S(2)}) %all-to-all-start.2) | async-done | bytes 8519712 | tf_op jit(solution)/shard_map/all_to_all | solution.py:254
  537.8 5.9 all-to-all-start.1
  543.7 19.9 %fusion.39 = f32[4,2,2,65,16,128]{5,4,3,1,0,2:T(8,128)S(1)} fusion(f32[65,32,8,2,128]{4,1,2,3,0:T(8,128)} %copy.59, pred[2,65,32,8,128]{4,2,3,1,0:T(8,128)(4,1)} %get-tuple-element.29, f32[32,8,1,1,4,16]{0,5,1,2,4,3:T(8,128)S(1)} %get-tuple-element.40, f32[32,8,1,1,4,16]{0,5,1,2,4,3:T(8,128)S(1)} %get-tuple-element.39, ...), kind=kOutput, calls=%fused_computation.54 | convolution fusion | flops 6551830528 | bytes 30015488 | tf_op jit(solution)/shard_map/bqwrck,wrcdsy->sbdqyk/dot_general | solution.py:253
  563.6 4.2 copy.60
  567.8 69.2 %all-to-all-done.1 = f32[4,2,2,65,16,128]{5,4,3,2,1,0:T(8,128)} async-done(((f32[4,2,2,65,16,128]{5,4,3,2,1,0:T(8,128)}), f32[4,2,2,65,16,128]{5,4,3,2,1,0:T(8,128)}, u32[]{:S(2)}, u32[]{:S(2)}) %all-to-all-start.1) | async-done | bytes 8519712 | tf_op jit(solution)/shard_map/all_to_all | solution.py:254
  637.0 5.6 all-to-all-start
  644.4 110.1 %psum.7 = f32[]{:T(128)} all-reduce(f32[]{:T(128)} %select_reduce_fusion.1), channel_id=1, replica_groups=mesh['particle'=4,'slab'=4,'half'=2] {'particle','slab'}, use_global_device_ids=true, to_apply=%region_2.3 | all-reduce | flops 1 | bytes 8 | tf_op jit(solution)/shard_map/psum | solution.py:179
  757.9 15.7 %fusion.60 = f32[2,256,16,2,128]{4,1,3,2,0:T(8,128)S(1)} fusion(f32[4,2,2,65,16,128,1]{5,4,3,2,1,0,6:T(8,128)} %bitcast.54, f32[4,65,1,2,256]{4,1,0,2,3:T(8,128)S(1)} %get-tuple-element.33, f32[4,65,1,2,256]{4,1,0,2,3:T(8,128)S(1)} %get-tuple-element.32), kind=kOutput, calls=%fused_computation.59 | convolution fusion | flops 6543380480 | bytes 17973248 | tf_op jit(solution)/shard_map/sbdqyk,sqdez->bzyek/dot_general | solution.py:255
  773.6 9.4 bitcast_add_fusion.refs_0_
  783.0 8.3 collective-permute-start.7
  791.3 15.7 %fusion.57 = f32[2,256,16,2,128]{4,1,3,2,0:T(8,128)S(1)} fusion(f32[4,2,2,65,16,128,1]{5,4,3,2,1,0,6:T(8,128)} %bitcast.42, f32[4,65,1,2,256]{4,1,0,2,3:T(8,128)S(1)} %get-tuple-element.33, f32[4,65,1,2,256]{4,1,0,2,3:T(8,128)S(1)} %get-tuple-element.32), kind=kOutput, calls=%fused_computation.58 | convolution fusion | flops 6543380480 | bytes 17973248 | tf_op jit(solution)/shard_map/sbdqyk,sqdez->bzyek/dot_general | solution.py:255
  807.0 9.4 bitcast_add_fusion.1.refs_0_
  816.5 16.2 %fusion.54 = f32[2,256,16,2,128]{4,1,3,2,0:T(8,128)S(1)} fusion(f32[4,2,2,65,16,128,1]{5,4,3,2,1,0,6:T(8,128)} %bitcast.24, f32[4,65,1,2,256]{4,1,0,2,3:T(8,128)S(1)} %get-tuple-element.33, f32[4,65,1,2,256]{4,1,0,2,3:T(8,128)S(1)} %get-tuple-element.32), kind=kOutput, calls=%fused_computation.57 | convolution fusion | flops 6543380480 | bytes 17973248 | tf_op jit(solution)/shard_map/sbdqyk,sqdez->bzyek/dot_general | solution.py:255
  832.7 8.0 bitcast_add_fusion.2.refs_0_
  841.3 8.8 fusion.67
  850.2 1.7 collective-permute-start.8
  851.9 7.2 fusion.69
  862.1 2.2 fusion.71
  865.4 1.9 collective-permute-start.3
  867.8 28.6 %collective-permute-done.8.refs_2_ = f32[2,256,1,256]{3,2,1,0:T(1,128)S(1)} collective-permute-done((f32[2,256,1,256]{3,2,1,0:T(1,128)S(1)}, f32[2,256,1,256]{3,2,1,0:T(1,128)S(1)}, u32[]{:S(2)}, u32[]{:S(2)}) %collective-permute-start.8) | collective-permute-done | bytes 524320 | tf_op jit(solution)/shard_map/ppermute | solution.py:262
  897.1 21.7 %shard_map.64 = (f32[256,16,256]{2,1,0:T(8,128)}, f32[256,16,256]{2,1,0:T(8,128)}) custom-call(f32[2,256,16,256]{3,2,1,0:T(8,128)} %bitcast_add_fusion.refs_0_, f32[2,256,16,256]{3,2,1,0:T(8,128)} %collective-permute-done.7.refs_1_, f32[2,256,1,256]{3,2,1,0:T(1,128)} %copy-done.9, f32[2,256,1,256]{3,2,1,0:T(1,128)} %copy-done.7), custom_call_target="tpu_custom_call" | custom-call | flops 41943040 | bytes 33554432 | tf_op jit(solution)/shard_map/pallas_call | solution.py:117
  919.9 26.2 %shard_map.65 = (f32[256,16,256]{2,1,0:T(8,128)}, f32[256,16,256]{2,1,0:T(8,128)}) custom-call(f32[2,256,16,256]{3,2,1,0:T(8,128)} %bitcast_add_fusion.1.refs_0_, f32[2,256,16,256]{3,2,1,0:T(8,128)} %collective-permute-done.4.refs_1_, f32[2,256,1,256]{3,2,1,0:T(1,128)} %copy-done.8, f32[2,256,1,256]{3,2,1,0:T(1,128)} %copy-done.6, ...), custom_call_target="tpu_custom_call" | custom-call | flops 41943040 | bytes 33554432 | tf_op jit(solution)/shard_map/pallas_call | solution.py:117
  946.1 25.7 %shard_map.66 = f32[256,16,256]{2,1,0:T(8,128)} custom-call(f32[2,256,16,256]{3,2,1,0:T(8,128)} %copy-done, f32[2,256,16,256]{3,2,1,0:T(8,128)} %copy-done.1, f32[2,256,1,256]{3,2,1,0:T(1,128)} %collective-permute-done.2.refs_2_, f32[2,256,1,256]{3,2,1,0:T(1,128)} %collective-permute-done.3.refs_3_, f32[256,16,256]{2,1,0:T(8,128)} %get-tuple-element.15.refs_4_, ...), custom_call_target="tpu_custom_call" | custom-call | flops 41943040 | bytes 33554432 | tf_op jit(solution)/shard_map/pallas_call | solution.py:117
  (100 shorter events, 19.8 us)
Async XLA Ops:
  6.5 6.1 copy-start.16
  6.5 176.2 %all-gather.3.cloned.1.call-start = ((), (), s32[]{:S(2)}) async-start(), calls=%async_computation.3 | async-start | bytes 11141120 | tf_op jit(solution)/shard_map/all_gather | solution.py:187
  9.8 4.7 copy-start.17
  9.8 4.7 copy-start.12
  9.8 4.9 copy-start.18
  14.8 0.6 copy-start.14
  19.0 4.8 copy-start.2
  22.1 56.2 %copy-start.19 = (s32[6]{0:T(128)S(1)}, s32[6]{0:T(128)}, u32[]{:S(2)}) copy-start(s32[6]{0:T(128)} %param.10) | copy-start | bytes 76
  26.2 314.5 %all-gather.5.cloned.1.call-start = ((), (), s32[]{:S(2)}) async-start(), calls=%async_computation.4 | async-start | bytes 11141120 | tf_op jit(solution)/shard_map/all_gather | solution.py:188
  26.3 50.6 %collective-permute-start = (f32[256,2176]{0,1:T(8,128)}, f32[256,2176]{0,1:T(8,128)S(1)}, u32[]{:S(2)}, u32[]{:S(2)}) collective-permute-start(f32[256,2176]{0,1:T(8,128)} %get-tuple-element.36), channel_id=1, source_target_pairs={{0,6},{2,4},{4,2},{6,0},{1,7},{3,5},{5,3},{7,1},{8,14},{10,12},{12... | collective-permute-start | bytes 6684680 | tf_op jit(solution)/shard_map/ppermute | solution.py:184
  76.9 1.3 copy-start.5
  78.3 0.6 copy-start.10
  345.6 8.1 copy-start.3
  351.1 2.6 copy-start.4
  438.6 99.3 %all-to-all-start.2 = ((f32[4,2,2,65,16,128]{5,4,3,2,1,0:T(8,128)}), f32[4,2,2,65,16,128]{5,4,3,2,1,0:T(8,128)}, u32[]{:S(2)}, u32[]{:S(2)}) async-start(f32[4,2,2,65,16,128]{5,4,3,2,1,0:T(8,128)} %copy.68), calls=%async_computation.2 | async-start | bytes 17039360 | tf_op jit(solution)/shard_map/all_to_all | solution.py:254
  537.8 99.1 %all-to-all-start.1 = ((f32[4,2,2,65,16,128]{5,4,3,2,1,0:T(8,128)}), f32[4,2,2,65,16,128]{5,4,3,2,1,0:T(8,128)}, u32[]{:S(2)}, u32[]{:S(2)}) async-start(f32[4,2,2,65,16,128]{5,4,3,2,1,0:T(8,128)} %copy.65), calls=%async_computation.1 | async-start | bytes 17039360 | tf_op jit(solution)/shard_map/all_to_all | solution.py:254
  567.8 76.0 %copy-start.13 = (s32[1,64,4]{1,2,0:T(4,128)S(1)}, s32[1,64,4]{1,2,0:T(4,128)}, u32[]{:S(2)}) copy-start(s32[1,64,4]{1,2,0:T(4,128)} %param.7) | copy-start | bytes 3076
  567.8 76.0 %copy-start.15 = (f32[64]{0:T(128)S(1)}, f32[64]{0:T(128)}, u32[]{:S(2)}) copy-start(f32[64]{0:T(128)} %copy-done.14) | copy-start | bytes 772
  567.8 189.3 %copy-start.11 = (s32[6]{0:T(128)S(1)}, s32[6]{0:T(128)}, u32[]{:S(2)}) copy-start(s32[6]{0:T(128)} %copy-done.10) | copy-start | bytes 76
  637.0 179.5 %all-to-all-start = ((f32[4,2,2,65,16,128]{5,4,3,2,1,0:T(8,128)}), f32[4,2,2,65,16,128]{5,4,3,2,1,0:T(8,128)}, u32[]{:S(2)}, u32[]{:S(2)}) async-start(f32[4,2,2,65,16,128]{5,4,3,2,1,0:T(8,128)} %copy.60), calls=%async_computation | async-start | bytes 17039360 | tf_op jit(solution)/shard_map/all_to_all | solution.py:254
  783.0 58.2 %collective-permute-start.7 = (f32[2,256,16,256]{3,2,1,0:T(8,128)}, f32[2,256,16,256]{3,2,1,0:T(8,128)}, u32[]{:S(2)}, u32[]{:S(2)}) collective-permute-start(f32[2,256,16,256]{3,2,1,0:T(8,128)} %bitcast_add_fusion.refs_0_), channel_id=1, source_target_pairs={{0,1},{1,0},{2,3},{3,2},{4,5},{5,4},{6,7},{7,6},{8,9},{9,8},{10,11... | collective-permute-start | bytes 25165832 | tf_op jit(solution)/shard_map/ppermute | solution.py:20
  816.5 35.4 %collective-permute-start.4 = (f32[2,256,16,256]{3,2,1,0:T(8,128)}, f32[2,256,16,256]{3,2,1,0:T(8,128)}, u32[]{:S(2)}, u32[]{:S(2)}) collective-permute-start(f32[2,256,16,256]{3,2,1,0:T(8,128)} %bitcast_add_fusion.1.refs_0_), channel_id=1, source_target_pairs={{0,1},{1,0},{2,3},{3,2},{4,5},{5,4},{6,7},{7,6},{8,9},{9,8},{10,11... | collective-permute-start | bytes 25165832 | tf_op jit(solution)/shard_map/ppermute | solution.py:20
  840.7 21.4 %copy-start = (f32[2,256,16,256]{3,2,1,0:T(8,128)}, f32[2,256,16,256]{3,2,1,0:T(8,128)S(1)}, u32[]{:S(2)}) copy-start(f32[2,256,16,256]{3,2,1,0:T(8,128)S(1)} %bitcast_add_fusion.2.refs_0_) | copy-start | bytes 25165828
  840.7 21.4 %collective-permute-start.1 = (f32[2,256,16,256]{3,2,1,0:T(8,128)S(1)}, f32[2,256,16,256]{3,2,1,0:T(8,128)S(1)}, u32[]{:S(2)}, u32[]{:S(2)}) collective-permute-start(f32[2,256,16,256]{3,2,1,0:T(8,128)S(1)} %bitcast_add_fusion.2.refs_0_), channel_id=1, source_target_pairs={{0,1},{1,0},{2,3},{3,2},{4,5},{5,4},{6,7},{7,6},{8,9},{9,8},{10,11... | collective-permute-start | bytes 25165832 | tf_op jit(solution)/shard_map/ppermute | solution.py:20
  850.1 17.1 %collective-permute-start.9 = (f32[2,256,1,256]{3,2,1,0:T(1,128)S(1)}, f32[2,256,1,256]{3,2,1,0:T(1,128)S(1)}, u32[]{:S(2)}, u32[]{:S(2)}) collective-permute-start(f32[2,256,1,256]{3,2,1,0:T(1,128)S(1)} %get-tuple-element.17), channel_id=1, source_target_pairs={{2,0},{4,2},{6,4},{8,6},{10,8},{12,10},{14,12},{16,14},{18,16},{20... | collective-permute-start | bytes 1572872 | tf_op jit(solution)/shard_map/ppermute | solution.py:263
  850.2 46.2 %collective-permute-start.8 = (f32[2,256,1,256]{3,2,1,0:T(1,128)S(1)}, f32[2,256,1,256]{3,2,1,0:T(1,128)S(1)}, u32[]{:S(2)}, u32[]{:S(2)}) collective-permute-start(f32[2,256,1,256]{3,2,1,0:T(1,128)S(1)} %get-tuple-element.18), channel_id=1, source_target_pairs={{0,2},{2,4},{4,6},{6,8},{8,10},{10,12},{12,14},{14,16},{16,18},{18... | collective-permute-start | bytes 1572872 | tf_op jit(solution)/shard_map/ppermute | solution.py:262
  859.1 59.7 %collective-permute-start.6 = (f32[2,256,1,256]{3,2,1,0:T(1,128)}, f32[2,256,1,256]{3,2,1,0:T(1,128)S(1)}, u32[]{:S(2)}, u32[]{:S(2)}) collective-permute-start(f32[2,256,1,256]{3,2,1,0:T(1,128)} %get-tuple-element.19), channel_id=1, source_target_pairs={{2,0},{4,2},{6,4},{8,6},{10,8},{12,10},{14,12},{16,14},{18,16},{20... | collective-permute-start | bytes 1572872 | tf_op jit(solution)/shard_map/ppermute | solution.py:263
  860.7 58.2 %collective-permute-start.5 = (f32[2,256,1,256]{3,2,1,0:T(1,128)S(1)}, f32[2,256,1,256]{3,2,1,0:T(1,128)S(1)}, u32[]{:S(2)}, u32[]{:S(2)}) collective-permute-start(f32[2,256,1,256]{3,2,1,0:T(1,128)S(1)} %get-tuple-element.20), channel_id=1, source_target_pairs={{0,2},{2,4},{4,6},{6,8},{8,10},{10,12},{12,14},{14,16},{16,18},{18... | collective-permute-start | bytes 1572872 | tf_op jit(solution)/shard_map/ppermute | solution.py:262
  862.1 3.3 copy-start.1
  865.4 80.7 %collective-permute-start.3 = (f32[2,256,1,256]{3,2,1,0:T(1,128)S(1)}, f32[2,256,1,256]{3,2,1,0:T(1,128)}, u32[]{:S(2)}, u32[]{:S(2)}) collective-permute-start(f32[2,256,1,256]{3,2,1,0:T(1,128)S(1)} %get-tuple-element.21), channel_id=1, source_target_pairs={{2,0},{4,2},{6,4},{8,6},{10,8},{12,10},{14,12},{16,14},{18,16},{20... | collective-permute-start | bytes 1572872 | tf_op jit(solution)/shard_map/ppermute | solution.py:263
  867.2 29.1 %copy-start.7 = (f32[2,256,1,256]{3,2,1,0:T(1,128)}, f32[2,256,1,256]{3,2,1,0:T(1,128)S(1)}, u32[]{:S(2)}) copy-start(f32[2,256,1,256]{3,2,1,0:T(1,128)S(1)} %collective-permute-done.9.refs_3_) | copy-start | bytes 1572868
  867.2 78.8 %collective-permute-start.2 = (f32[2,256,1,256]{3,2,1,0:T(1,128)S(1)}, f32[2,256,1,256]{3,2,1,0:T(1,128)}, u32[]{:S(2)}, u32[]{:S(2)}) collective-permute-start(f32[2,256,1,256]{3,2,1,0:T(1,128)S(1)} %get-tuple-element.22), channel_id=1, source_target_pairs={{0,2},{2,4},{4,6},{6,8},{8,10},{10,12},{12,14},{14,16},{16,18},{18... | collective-permute-start | bytes 1572872 | tf_op jit(solution)/shard_map/ppermute | solution.py:262
  896.3 0.8 copy-start.9
  918.9 0.8 copy-start.6
  918.9 1.0 copy-start.8
Sparse Core Ops, SparseCore 0:
  26.4 156.3 all-gather.2
  184.3 156.3 all-gather.4

commit v2 on v1

--- a/solution.py
+++ b/solution.py
@@ -11,6 +11,7 @@
 BOX = 256
 TILE_ROWS = 8
 CHUNK_BANDS = 2
+COL_PARTS = 2
 
 error_floor = 1.0
 high = lax.Precision.HIGH
@@ -44,7 +45,7 @@
     else:
         num_ref, den_ref, padded, smooth = outs
     band = pl.program_id(0)
-    depth, rows, width = own_ref.shape[1:]
+    depth, rows, width = own_ref.shape
 
     @pl.when(band == 0)
     def _():
@@ -57,10 +58,10 @@
 
     def smooth_rows(step, carry):
         here = pl.ds(step * step_planes, step_planes)
-        gap = own_ref[0, here] - other_ref[0, here]
-        padded[:, 0:1, :] = low_ref[0, here]
+        gap = own_ref[here] - other_ref[here]
+        padded[:, 0:1, :] = low_ref[here]
         padded[:, 1 : rows + 1, :] = gap * gap
-        padded[:, rows + 1 : rows + 2, :] = high_ref[0, here]
+        padded[:, rows + 1 : rows + 2, :] = high_ref[here]
         total = (
             padded[:, 0:rows, :] + padded[:, 1 : rows + 1, :] + padded[:, 2 : rows + 2, :]
         )
@@ -81,7 +82,7 @@
             + smooth[pl.ds(start + 2, step_planes)]
         )
         weight = 1.0 / (total * (1.0 / 27.0) + error_floor)
-        num_ref[here] += weight * own_ref[0, here]
+        num_ref[here] += weight * own_ref[here]
         den_ref[here] += weight
         return carry
 
@@ -99,12 +100,13 @@
             lax.fori_loop(0, depth // step_planes, divide, 0)
 
 
-def blend(own, other, low, high_rows, sums, last):
-    bands, depth, rows, width = own.shape
+def blend(own, other, low, high_rows, sums, bands, last):
+    depth, rows, width = own.shape
+    width = width // bands
     first = sums is None
     step_planes = 8
-    map_spec = pl.BlockSpec((1, depth, rows, width), lambda b: (b, 0, 0, 0))
-    row_spec = pl.BlockSpec((1, depth, 1, width), lambda b: (b, 0, 0, 0))
+    map_spec = pl.BlockSpec((depth, rows, width), lambda b: (0, 0, b))
+    row_spec = pl.BlockSpec((depth, 1, width), lambda b: (0, 0, b))
     whole = pl.BlockSpec((depth, rows, width), lambda b: (0, 0, 0))
     kept = jax.ShapeDtypeStruct((depth, rows, width), jnp.float32)
     scratch = [
@@ -164,29 +166,49 @@
     upper = parts[:, :, :, half_box:]
     turn = lax.broadcasted_iota(jnp.int32, (half_box, half_box), 0)
     target = lax.broadcasted_iota(jnp.int32, (half_box, half_box), 1)
-    swap = jnp.where((turn + target == half_box) & (target > 0), 1.0, 0.0).astype(jnp.bfloat16)
+    swap = jnp.where((turn + target) % half_box == 0, 1.0, 0.0).astype(jnp.bfloat16)
     mirrored = jnp.einsum(
         "ercx,xk->erck", upper.astype(jnp.bfloat16), swap, preferred_element_type=jnp.float32
     )
-    mirrored = mirrored * jnp.array([1.0, -1.0], jnp.float32)[:, None]
+    col_freq = jnp.arange(half_box, dtype=jnp.int32)
+    tile_rows = jnp.arange(TILE_ROWS, dtype=jnp.int32)
+    is_lone = (entry_slot == 0) & (slab_pos == 0)
+    is_first = (tile_rows[:, None] == 0) & (jnp.arange(2, dtype=jnp.int32) == 0)
+    keep = (col_freq > 0) | (is_lone[:, None, None, None] & is_first[None, :, :, None])
+    mirrored = jnp.where(keep, mirrored, 0.0) * jnp.array([1.0, -1.0], jnp.float32)[:, None]
     mirrored = jnp.concatenate([mirrored[:, :1], mirrored[:, :0:-1]], axis=1)
 
-    lone = jnp.sum(
-        jnp.where(
-            (entry_slot == 0) & (slab_pos == 0), entry_gain * parts[:, 0, 0, half_box], 0.0
-        )
-    )
-    lone = lax.psum(lone, ("particle", "slab"))
-
-    width = 2 * TILE_ROWS * half_box
-    send_direct = jnp.concatenate([direct.reshape(entries, width), notes], axis=1)
-    send_mirror = jnp.concatenate([mirrored.reshape(entries, width), notes], axis=1)
-    send_mirror = lax.ppermute(
-        send_mirror, "slab", [(i, slab_count - 1 - i) for i in range(slab_count)]
-    )
-    all_direct = lax.all_gather(send_direct, "particle", axis=0, tiled=True)
-    all_mirror = lax.all_gather(send_mirror, "particle", axis=0, tiled=True)
-    all_direct, all_mirror = lax.optimization_barrier((all_direct, all_mirror))
+    span = half_box // COL_PARTS
+    width = 2 * TILE_ROWS * span
+    flip = [(i, slab_count - 1 - i) for i in range(slab_count)]
+
+    def columns(array, part):
+        cut = array[..., part * span : (part + 1) * span].reshape(entries, width)
+        return cut * 2.0
+
+    def gather(array):
+        return lax.all_gather(array, "particle", axis=0, tiled=True)
+
+    sent_direct = jnp.concatenate([columns(direct, 0), notes], axis=1)
+    sent_mirror = lax.ppermute(
+        jnp.concatenate([columns(mirrored, 0), notes], axis=1), "slab", flip
+    )
+    late_mirror = lax.ppermute(
+        jnp.concatenate([columns(mirrored, part) for part in range(1, COL_PARTS)], axis=1),
+        "slab",
+        flip,
+    )
+    all_direct = gather(sent_direct)
+    sent_mirror, all_direct = lax.optimization_barrier((sent_mirror, all_direct))
+    all_mirror = gather(sent_mirror)
+    gathered = [(all_direct[:, :width], all_mirror[:, :width])]
+    for part in range(1, COL_PARTS):
+        late = jnp.concatenate(
+            [columns(direct, part), late_mirror[:, (part - 1) * width : part * width]], axis=1
+        )
+        late, all_mirror = lax.optimization_barrier((late, all_mirror))
+        late = lax.optimization_barrier(gather(late))
+        gathered.append((late[:, :width], late[:, width:]))
 
     slot_ids = jnp.arange(slot_count, dtype=jnp.int32)
     slot_d = all_direct[:, width].astype(jnp.int32)
@@ -203,65 +225,91 @@
             jnp.bfloat16
         )
 
-    values = jnp.concatenate([all_direct[:, :width], all_mirror[:, :width]], axis=0).astype(
-        jnp.bfloat16
-    )
-    row_width = 2 * half_box
-    first_rows = jnp.dot(
-        placing(jnp.concatenate([slot_d, slot_m0])),
-        values[:, :row_width],
-        preferred_element_type=jnp.float32,
-    )
-    other_rows = jnp.dot(
-        placing(jnp.concatenate([slot_d, slot_m1])),
-        values[:, row_width:],
-        preferred_element_type=jnp.float32,
-    )
-    spectrum = jnp.concatenate([first_rows, other_rows], axis=1).reshape(
-        planes, blocks, TILE_ROWS, 2, half_box
-    )
-
-    col_freq = jnp.arange(half_box, dtype=jnp.int32)
+    place_first = placing(jnp.concatenate([slot_d, slot_m0]))
+    place_other = placing(jnp.concatenate([slot_d, slot_m1]))
+
     positions = jnp.arange(BOX, dtype=jnp.int32)
-    row_freq = positions.reshape(blocks, TILE_ROWS)
+    row_freq = positions.reshape(blocks, TILE_ROWS).T
     plane_freq = slab_pos * slab_depth + jnp.arange(planes, dtype=jnp.int32)
     plane_sq = signed_wave(plane_freq, BOX) ** 2
     row_sq = signed_wave(row_freq, BOX) ** 2
-    radius = plane_sq[:, None, None, None] + row_sq[None, :, :, None] + col_freq**2
-
     row_table = turn_table(
         row_freq, group_pos * group_rows + jnp.arange(group_rows, dtype=jnp.int32), BOX
     )
-    row_table = row_table.reshape(blocks, TILE_ROWS, 2, 2, slab_count, rows_here)
+    row_table = row_table.reshape(TILE_ROWS, blocks, 2, 2, slab_count, rows_here)
     every_plane = (
         jnp.arange(slab_count, dtype=jnp.int32)[:, None] * slab_depth
         + jnp.arange(planes, dtype=jnp.int32)
     )
     plane_table = turn_table(every_plane, positions, BOX)
     col_table = turn_table(col_freq, positions, BOX)[:, :, 0] / BOX
-    sign = jnp.where(positions % 2 == 0, 1.0 / BOX, -1.0 / BOX)
+    same_band = jnp.eye(CHUNK_BANDS, dtype=jnp.float32)
+    swing = jnp.where(positions % 2 == 0, 0.0, -2.0 / BOX)
 
     bands = cutoffs.shape[0]
+    starts = range(0, bands, CHUNK_BANDS)
     around = slab_count * group_count
     forward = [(i, (i + 1) % around) for i in range(around)]
     backward = [((i + 1) % around, i) for i in range(around)]
+    maps = {}
     sums = None
-    for start in range(0, bands, CHUNK_BANDS):
-        limit = (cutoffs * cutoffs)[start : start + CHUNK_BANDS]
-        inside = radius[None] <= limit[:, None, None, None, None]
-        masked = jnp.where(inside[:, :, :, :, None, :], spectrum[None], 0.0)
-        rows_done = jnp.einsum("bqwrck,wrcdsy->sbdqyk", masked, row_table, precision=high)
-        arrived = lax.all_to_all(rows_done, "slab", split_axis=0, concat_axis=0, tiled=True)
-        planes_done = jnp.einsum("sbdqyk,sqdez->bzyek", arrived, plane_table, precision=high)
-        filtered = jnp.einsum("bzyek,kex->bzyx", planes_done, col_table, precision=high)
-        extra = jnp.where(limit >= half_box * half_box, lone, 0.0)
-        filtered = filtered + extra[:, None, None, None] * sign
-        other = from_partner(filtered, "half", 0)
-        head = (filtered[:, :, :1] - other[:, :, :1]) ** 2
-        tail = (filtered[:, :, -1:] - other[:, :, -1:]) ** 2
-        low = lax.ppermute(tail, ("particle", "slab"), forward)
-        high_rows = lax.ppermute(head, ("particle", "slab"), backward)
-        sums = blend(filtered, other, low, high_rows, sums, start + CHUNK_BANDS >= bands)
+    before = []
+    for part in range(COL_PARTS):
+        values = (jnp.concatenate(gathered[part], axis=0) * 0.5).astype(jnp.bfloat16)
+        values = values.reshape(-1, TILE_ROWS, 2, 1, span)
+        values = jnp.broadcast_to(values, values.shape[:3] + (CHUNK_BANDS, span))
+        values = values.reshape(-1, TILE_ROWS, 2, CHUNK_BANDS * span)
+        first_rows = jnp.einsum(
+            "te,erck->rctk", place_first, values[:, :1], preferred_element_type=jnp.float32
+        )
+        other_rows = jnp.einsum(
+            "te,erck->rctk", place_other, values[:, 1:], preferred_element_type=jnp.float32
+        )
+        spectrum = jnp.concatenate([first_rows, other_rows], axis=0).reshape(
+            TILE_ROWS, 2, planes, blocks, CHUNK_BANDS * span
+        )
+        cols = col_freq[part * span : (part + 1) * span]
+        lanes = jnp.tile(cols, CHUNK_BANDS)
+        radius = plane_sq[:, None, None] + row_sq[:, None, :, None] + lanes**2
+        lone_place = (slab_pos == slab_count - 1) & (
+            (jnp.arange(planes) == slab_depth)[:, None, None] & (lanes == 0)
+        )
+        radius = jnp.where(lone_place, half_box * half_box, radius)
+        part_table = jnp.einsum(
+            "kex,bf->ebkfx", col_table[part * span : (part + 1) * span], same_band, precision=lax.Precision.HIGHEST
+        )
+        part_table = part_table.reshape(2 * CHUNK_BANDS * span, CHUNK_BANDS * BOX)
+        for start in starts:
+            limit = (cutoffs * cutoffs)[start : start + CHUNK_BANDS]
+            inside = radius <= jnp.repeat(limit, span)
+            masked = jnp.where(inside[:, None], spectrum, 0.0)
+            rows_done = jnp.einsum("rcqwl,rwcdsy->sdqyl", masked, row_table, precision=high)
+            if len(before) > 1:
+                rows_done, _ = lax.optimization_barrier((rows_done, before[-2]))
+            arrived = lax.all_to_all(rows_done, "slab", split_axis=0, concat_axis=0, tiled=True)
+            if sums is not None:
+                arrived, sums = lax.optimization_barrier((arrived, sums))
+            planes_done = jnp.einsum("sdqyl,sqdez->zyel", arrived, plane_table, precision=high)
+            planes_done = planes_done.reshape(BOX, rows_here, 2 * CHUNK_BANDS * span)
+            filtered = jnp.einsum("zyl,lx->zyx", planes_done, part_table, precision=high)
+            if part == 0:
+                lone = arrived[slab_count - 1, 0, slab_depth, 0].reshape(CHUNK_BANDS, span)[:, 0]
+                filtered = filtered + (lone[:, None] * swing).reshape(-1)
+            else:
+                filtered = filtered + maps[start]
+            maps[start] = filtered
+            if part < COL_PARTS - 1:
+                before.append(filtered)
+                continue
+            other = from_partner(filtered, "half", 0)
+            head = (filtered[:, :1] - other[:, :1]) ** 2
+            tail = (filtered[:, -1:] - other[:, -1:]) ** 2
+            low = lax.ppermute(tail, ("particle", "slab"), forward)
+            high_rows = lax.ppermute(head, ("particle", "slab"), backward)
+            sums = blend(
+                filtered, other, low, high_rows, sums, CHUNK_BANDS, start + CHUNK_BANDS >= bands
+            )
+            before.append(filtered)
     return sums[None]
 
 

time: 991 us -> 961 us (0.970)
  waiting for transfers between devices: 465 us -> 388 us
  matrix products: 156 us -> 220 us
  blocking collectives: 110 us -> 51.2 us
  local copies, waits for them, and re-layouts: 74.4 us -> 101 us
  starting transfers between devices: 35.7 us -> 47.6 us
    all_gather x2 -> x3, waiting for transfers between devices: 249 us -> 120 us  [gather(): return lax.all_gather(array, 'particle', axis=0, tiled=True)]
    psum x1 -> x0, blocking collectives: 110 us -> none  [on_device(): lone = lax.psum(lone, ('particle', 'slab'))]
    ppermute x3, waiting for transfers between devices: 0.01 us -> 109 us  [on_device(): high_rows = lax.ppermute(head, ('particle', 'slab'), backward)]
    dot_general x11 -> x22, matrix products: 156 us -> 219 us  [the longest x6 77.3 us: on_device(): jnp.einsum('rcqwl,rwcdsy->sdqyl', masked, row_table, precision=high)]
    all_to_all x3 -> x5, waiting for transfers between devices: 139 us -> 82.4 us  [on_device(): lax.all_to_all(rows_done, 'slab', split_axis=0, concat_axis=0, tiled=True)]
    all_to_all x0 -> x1, blocking collectives: none -> 51.2 us  [on_device(): lax.all_to_all(rows_done, 'slab', split_axis=0, concat_axis=0, tiled=True)]
    reshape x0 -> x8, local copies, waits for them, and re-layouts: none -> 33.9 us  [the longest x6 33 us: on_device(): planes_done = planes_done.reshape(BOX, rows_here, 2 * CHUNK_BANDS * span)]
    broadcast_in_dim x2 -> x5, local copies, waits for them, and re-layouts: 35.3 us -> 11.4 us  [the longest x2 11.2 us: on_device(): values = jnp.broadcast_to(values, values.shape[:3] + (CHUNK_BANDS, span))]
  transfers between devices with their start and end apart: 15 -> 19, of which waited for: 6 -> 14; matrix products, arithmetic and copies ran while one was open for 16% -> 23% of each run, Pallas kernels for 5% -> 5%
where the time goes in v2:
time: 961 us; the launch traced here: 952 us
  waiting for transfers between devices  388 us (40%)
  matrix products  220 us (23%)
  local copies, waits for them, and re-layouts  101 us (11%)
  Pallas kernels  71.1 us (7%)
  other arithmetic  59.1 us (6%)
  blocking collectives  51.2 us (5%)
  starting transfers between devices  47.6 us (5%)
  between operations  14.1 us (1%)
    all_gather x3, waiting for transfers between devices, gather(): return lax.all_gather(array, 'particle', axis=0, tiled=True)  120 us
    ppermute x3, waiting for transfers between devices, on_device(): high_rows = lax.ppermute(head, ('particle', 'slab'), backward)  109 us
    all_to_all x5, waiting for transfers between devices, on_device(): lax.all_to_all(rows_done, 'slab', split_axis=0, concat_axis=0, tiled=True)  82.4 us
    dot_general x6, matrix products, on_device(): jnp.einsum('rcqwl,rwcdsy->sdqyl', masked, row_table, precision=high)  77.3 us
    pallas_call x3, Pallas kernels, blend(): pl.pallas_call(functools.partial(blend_kernel, first, last, step_planes),...  71.1 us
    dot_general x6, matrix products, on_device(): jnp.einsum('zyl,lx->zyx', planes_done, part_table, precision=high)  51.6 us
    all_to_all x1, blocking collectives, on_device(): lax.all_to_all(rows_done, 'slab', split_axis=0, concat_axis=0, tiled=True)  51.2 us
    dot_general x6, matrix products, on_device(): jnp.einsum('sdqyl,sqdez->zyel', arrived, plane_table, precision=high)  44.6 us
  transfers between devices with their start and end apart: 19, of which 14 were waited for; matrix products, arithmetic and copies ran while one was open for 23% of the time, Pallas kernels for 5%

profile of v2, /device:TPU:25, one launch (start us, length us, event | category | flops | bytes accessed | tf_op | source)
XLA Modules:
  0.0 952.3 jit_solution(257320192223600741)
XLA Ops:
  28.8 25.7 %collective-permute-done.1 = f32[256,1152]{0,1:T(8,128)} collective-permute-done((f32[256,1152]{0,1:T(8,128)S(1)}, f32[256,1152]{0,1:T(8,128)}, u32[]{:S(2)}, u32[]{:S(2)}) %collective-permute-start.1) | collective-permute-done | bytes 1179680 | tf_op jit(solution)/shard_map/ppermute | solution.py:193
  54.5 60.0 %all-gather.4.cloned.1.call-done = f32[1024,1152]{0,1:T(8,128)} async-done(((f32[256,1152]{0,1:T(8,128)}), f32[1024,1152]{0,1:T(8,128)}) %all-gather.4.cloned.1.call-update) | async-done | bytes 4718608 | tf_op jit(solution)/shard_map/all_gather | solution.py:190
  118.5 10.8 %fusion.34 = (pred[8,65,32,128]{3,2,0,1:T(8,128)(4,1)}, pred[8,65,32,128]{3,2,0,1:T(8,128)(4,1)}, pred[8,65,32,128]{3,2,0,1:T(8,128)(4,1)}, pred[8,65,32,128]{3,...) fusion(s32[128]{0:T(128)S(1)} %le.78, s32[128]{0:T(128)S(1)} %integer_pow.59, ...), kind=kLoop, calls=%fused_computation.39 | loop fusion | flops 21299200 | bytes 12865280 | tf_op jit(solution)/shard_map/le | solution.py:284
  130.5 9.8 %collective-permute-done = f32[256,1024]{0,1:T(8,128)S(1)} collective-permute-done((f32[256,1024]{0,1:T(8,128)}, f32[256,1024]{0,1:T(8,128)S(1)}, u32[]{:S(2)}, u32[]{:S(2)}) %collective-permute-start) | collective-permute-done | bytes 1048608 | tf_op jit(solution)/shard_map/ppermute | solution.py:196
  144.0 60.0 %all-gather.6.cloned.1.call-done = f32[1024,1152]{0,1:T(8,128)} async-done(((f32[256,1152]{0,1:T(8,128)}), f32[1024,1152]{0,1:T(8,128)}) %all-gather.6.cloned.1.call-update) | async-done | bytes 4718608 | tf_op jit(solution)/shard_map/all_gather | solution.py:190
  217.9 18.9 %convolution_bitcast_fusion = f32[7,2,2080,128]{3,2,1,0:T(8,128)} fusion(s32[2048]{0:T(1024)S(1)} %get-tuple-element.78, bf16[2048]{0:T(1024)(128)(2,1)S(1)} %pad_maximum_fusion.7, bf16[2048,8,2,128]{0,3,2,1:T(8,128)(2,1)S(1)} %bitcast.299), kind=kOutput, calls=%fused_computation.30 | convolution fusion | flops 15275786240 | bytes 22261760 | tf_op jit(solution)/shard_map/te,erck->rctk/dot_general | solution.py:265
  236.7 6.5 pad_maximum_fusion.1
  243.2 8.2 fusion.96
  258.8 15.3 %fusion.99 = f32[4,2,65,16,128]{4,3,2,0,1:T(8,128)S(1)} fusion(f32[8,2,65,32,128]{4,3,2,1,0:T(8,128)} %bitcast.278, pred[8,65,32,128]{3,2,0,1:T(8,128)(4,1)S(1)} %copy-done.11, f32[8,32,1,1,4,16]{1,5,0,2,4,3:T(8,128)S(1)} %copy-done.20, f32[8,32,1,1,4,16]{1,5,0,2,4,3:T(8,128)S(1)} %get-tuple-element.75, f32[8,32,1,1,4,16]{1,5,0,2,4,3:T(8,128)S(1)} %get-tuple-element.74), kind=kOutput, calls=%fused_computation.103 | convolution fusion | flops 3276013568 | bytes 23625728 | tf_op jit(solution)/shard_map/rcqwl,rwcdsy->sdqyl/dot_general | solution.py:286
  276.5 30.1 %all-to-all-done = f32[4,2,65,16,128]{4,3,2,1,0:T(8,128)} async-done(((f32[4,2,65,16,128]{4,3,2,1,0:T(8,128)}), f32[4,2,65,16,128]{4,3,2,1,0:T(8,128)}, u32[]{:S(2)}, u32[]{:S(2)}) %all-to-all-start) | async-done | bytes 4259872 | tf_op jit(solution)/shard_map/all_to_all | solution.py:289
  315.3 7.7 fusion.108
  330.8 28.6 %all-to-all-done.2 = f32[4,2,65,16,128]{4,3,2,1,0:T(8,128)} async-done(((f32[4,2,65,16,128]{4,3,2,1,0:T(8,128)}), f32[4,2,65,16,128]{4,3,2,1,0:T(8,128)}, u32[]{:S(2)}, u32[]{:S(2)}) %all-to-all-start.2) | async-done | bytes 4259872 | tf_op jit(solution)/shard_map/all_to_all | solution.py:289
  360.6 8.0 broadcast_add_fusion.2
  375.7 6.8 broadcast_in_dim.236
  386.3 18.9 %convolution_bitcast_fusion.1 = f32[7,2,2080,128]{3,2,1,0:T(8,128)} fusion(s32[2048]{0:T(1024)S(1)} %get-tuple-element.78, bf16[2048]{0:T(1024)(128)(2,1)S(1)} %pad_maximum_fusion.7, bf16[2048,8,2,128]{0,3,2,1:T(8,128)(2,1)S(1)} %bitcast.297), kind=kOutput, calls=%fused_computation.31 | convolution fusion | flops 15275786240 | bytes 22261760 | tf_op jit(solution)/shard_map/te,erck->rctk/dot_general | solution.py:265
  405.2 6.7 pad_maximum_fusion
  411.9 8.2 fusion.93
  428.1 7.7 fusion.114
  438.1 5.5 copy.236
  443.7 7.9 broadcast_add_fusion.1
  451.6 23.6 %all-to-all-done.1 = f32[4,2,65,16,128]{4,3,2,1,0:T(8,128)} async-done(((f32[4,2,65,16,128]{4,3,2,1,0:T(8,128)}), f32[4,2,65,16,128]{4,3,2,1,0:T(8,128)}, u32[]{:S(2)}, u32[]{:S(2)}) %all-to-all-start.1) | async-done | bytes 4259872 | tf_op jit(solution)/shard_map/all_to_all | solution.py:289
  475.3 7.7 fusion.111
  485.3 5.5 copy.231
  490.8 9.4 convolution_add_fusion.2.refs_0_
  501.6 15.2 %fusion.105 = f32[4,2,65,16,128]{4,3,2,0,1:T(8,128)S(1)} fusion(f32[8,2,65,32,128]{4,3,2,1,0:T(8,128)} %bitcast.279, pred[8,65,32,128]{3,2,0,1:T(8,128)(4,1)S(1)} %copy-done.9, f32[8,32,1,1,4,16]{1,5,0,2,4,3:T(8,128)S(1)} %copy-done.22, f32[8,32,1,1,4,16]{1,5,0,2,4,3:T(8,128)S(1)} %get-tuple-element.75, f32[8,32,1,1,4,16]{1,5,0,2,4,3:T(8,128)S(1)} %get-tuple-element.74), kind=kOutput, calls=%fused_computation.105 | convolution fusion | flops 3276013568 | bytes 23625728 | tf_op jit(solution)/shard_map/rcqwl,rwcdsy->sdqyl/dot_general | solution.py:286
  517.4 51.2 %all_to_all.30 = f32[4,2,65,16,128]{4,3,2,1,0:T(8,128)S(1)} all-to-all(f32[4,2,65,16,128]{4,3,2,1,0:T(8,128)S(1)} %copy.202), channel_id=1, replica_groups=mesh['particle'=4,'slab'=4,'half'=2] {'slab'}, dimensions={0} | all-to-all | bytes 8519680 | tf_op jit(solution)/shard_map/all_to_all | solution.py:289
  570.5 6.3 fusion.117
  585.5 8.0 broadcast_add_fusion
  593.5 15.2 %fusion.102 = f32[4,2,65,16,128]{4,3,2,0,1:T(8,128)S(1)} fusion(f32[8,2,65,32,128]{4,3,2,1,0:T(8,128)} %bitcast.281, pred[8,65,32,128]{3,2,0,1:T(8,128)(4,1)S(1)} %copy-done.8, f32[8,32,1,1,4,16]{1,5,0,2,4,3:T(8,128)S(1)} %copy-done.22, f32[8,32,1,1,4,16]{1,5,0,2,4,3:T(8,128)S(1)} %get-tuple-element.75, f32[8,32,1,1,4,16]{1,5,0,2,4,3:T(8,128)S(1)} %get-tuple-element.74), kind=kOutput, calls=%fused_computation.104 | convolution fusion | flops 3276013568 | bytes 23625728 | tf_op jit(solution)/shard_map/rcqwl,rwcdsy->sdqyl/dot_general | solution.py:286
  616.3 6.9 fusion.135
  626.2 48.2 %collective-permute-done.4.refs_3_ = f32[256,1,512]{2,1,0:T(1,128)S(1)} collective-permute-done((f32[256,1,512]{2,1,0:T(1,128)S(1)}, f32[256,1,512]{2,1,0:T(1,128)S(1)}, u32[]{:S(2)}, u32[]{:S(2)}) %collective-permute-start.4) | collective-permute-done | bytes 524320 | tf_op jit(solution)/shard_map/ppermute | solution.py:308
  674.5 9.2 collective-permute-done.3.refs_2_
  684.5 21.3 %shard_map.64 = (f32[256,16,256]{2,1,0:T(8,128)}, f32[256,16,256]{2,1,0:T(8,128)}) custom-call(f32[256,16,512]{2,1,0:T(8,128)} %convolution_add_fusion.2.refs_0_, f32[256,16,512]{2,1,0:T(8,128)} %collective-permute-done.2.refs_1_, f32[256,1,512]{2,1,0:T(1,128)} %copy-done.16, f32[256,1,512]{2,1,0:T(1,128)} %copy-done.14), custom_call_target="tpu_custom_call" | custom-call | flops 41943040 | bytes 33554432 | tf_op jit(solution)/shard_map/pallas_call | solution.py:119
  705.8 7.7 fusion.120
  715.9 5.5 copy.246
  721.4 9.4 convolution_add_fusion.1.refs_0_
  732.7 15.2 %fusion.90 = f32[4,2,65,16,128]{4,3,2,0,1:T(8,128)S(1)} fusion(f32[8,2,65,32,128]{4,3,2,1,0:T(8,128)} %bitcast.282, pred[8,65,32,128]{3,2,0,1:T(8,128)(4,1)S(1)} %copy-done.7, f32[8,32,1,1,4,16]{1,5,0,2,4,3:T(8,128)S(1)} %copy-done.22, f32[8,32,1,1,4,16]{1,5,0,2,4,3:T(8,128)S(1)} %get-tuple-element.75, f32[8,32,1,1,4,16]{1,5,0,2,4,3:T(8,128)S(1)} %get-tuple-element.74), kind=kOutput, calls=%fused_computation.100 | convolution fusion | flops 3276013568 | bytes 23625728 | tf_op jit(solution)/shard_map/rcqwl,rwcdsy->sdqyl/dot_general | solution.py:286
  755.8 7.0 fusion.133
  766.2 49.3 %collective-permute-done.7.refs_3_ = f32[256,1,512]{2,1,0:T(1,128)S(1)} collective-permute-done((f32[256,1,512]{2,1,0:T(1,128)S(1)}, f32[256,1,512]{2,1,0:T(1,128)S(1)}, u32[]{:S(2)}, u32[]{:S(2)}) %collective-permute-start.7) | collective-permute-done | bytes 524320 | tf_op jit(solution)/shard_map/ppermute | solution.py:308
  815.5 8.8 collective-permute-done.6.refs_2_
  825.1 25.2 %shard_map.65 = (f32[256,16,256]{2,1,0:T(8,128)}, f32[256,16,256]{2,1,0:T(8,128)}) custom-call(f32[256,16,512]{2,1,0:T(8,128)} %convolution_add_fusion.1.refs_0_, f32[256,16,512]{2,1,0:T(8,128)} %collective-permute-done.5.refs_1_, f32[256,1,512]{2,1,0:T(1,128)} %copy-done.15, f32[256,1,512]{2,1,0:T(1,128)} %copy-done.13, ...), custom_call_target="tpu_custom_call" | custom-call | flops 41943040 | bytes 33554432 | tf_op jit(solution)/shard_map/pallas_call | solution.py:119
  850.3 7.7 fusion.123
  865.8 8.8 convolution_add_fusion.refs_0_
  875.5 12.8 %collective-permute-done.8.refs_1_ = f32[256,16,512]{2,1,0:T(8,128)S(1)} collective-permute-done((f32[256,16,512]{2,1,0:T(8,128)S(1)}, f32[256,16,512]{2,1,0:T(8,128)S(1)}, u32[]{:S(2)}, u32[]{:S(2)}) %collective-permute-start.8) | collective-permute-done | bytes 8388640 | tf_op jit(solution)/shard_map/ppermute | solution.py:21
  892.0 6.0 collective-permute-start.10
  898.0 11.0 %collective-permute-done.10.refs_3_ = f32[256,1,512]{2,1,0:T(1,128)S(1)} collective-permute-done((f32[256,1,512]{2,1,0:T(1,128)S(1)}, f32[256,1,512]{2,1,0:T(1,128)S(1)}, u32[]{:S(2)}, u32[]{:S(2)}) %collective-permute-start.10) | collective-permute-done | bytes 524320 | tf_op jit(solution)/shard_map/ppermute | solution.py:308
  909.0 11.2 %collective-permute-done.9.refs_2_ = f32[256,1,512]{2,1,0:T(1,128)S(1)} collective-permute-done((f32[256,1,512]{2,1,0:T(1,128)S(1)}, f32[256,1,512]{2,1,0:T(1,128)S(1)}, u32[]{:S(2)}, u32[]{:S(2)}) %collective-permute-start.9) | collective-permute-done | bytes 524320 | tf_op jit(solution)/shard_map/ppermute | solution.py:307
  921.0 24.5 %shard_map.66 = f32[256,16,256]{2,1,0:T(8,128)} custom-call(f32[256,16,512]{2,1,0:T(8,128)} %copy-done, f32[256,16,512]{2,1,0:T(8,128)} %copy-done.4, f32[256,1,512]{2,1,0:T(1,128)} %copy-done.18, f32[256,1,512]{2,1,0:T(1,128)} %copy-done.17, f32[256,16,256]{2,1,0:T(8,128)} %get-tuple-element.39.refs_4_, f32[256,16,256]{2,1,0:T(8,128)} %get-tuple-element.40.refs_5_), custom_call_target="tpu_custom_call" | custom-call | flops 41943040 | bytes 33554432 | tf_op jit(solution)/shard_map/pallas_call | solution.py:119
  (206 shorter events, 149.2 us)
Async XLA Ops:
  6.5 9.3 copy-start.28
  6.5 108.0 %all-gather.4.cloned.1.call-start = ((), (), s32[]{:S(2)}) async-start(), calls=%async_computation.6 | async-start | bytes 5898240 | tf_op jit(solution)/shard_map/all_gather | solution.py:190
  16.3 3.9 copy-start.25
  16.3 4.1 copy-start.26
  25.3 92.4 %copy-start.27 = (s32[6]{0:T(128)S(1)}, s32[6]{0:T(128)}, u32[]{:S(2)}) copy-start(s32[6]{0:T(128)} %param.10) | copy-start | bytes 76
  26.6 177.4 %all-gather.6.cloned.1.call-start = ((), (), s32[]{:S(2)}) async-start(), calls=%async_computation.7 | async-start | bytes 5898240 | tf_op jit(solution)/shard_map/all_gather | solution.py:190
  26.6 27.9 %collective-permute-start.1 = (f32[256,1152]{0,1:T(8,128)S(1)}, f32[256,1152]{0,1:T(8,128)}, u32[]{:S(2)}, u32[]{:S(2)}) collective-permute-start(f32[256,1152]{0,1:T(8,128)S(1)} %get-tuple-element.73), channel_id=1, source_target_pairs={{0,6},{2,4},{4,2},{6,0},{1,7},{3,5},{5,3},{7,1},{8,14},{10,12},{12... | collective-permute-start | bytes 3538952 | tf_op jit(solution)/shard_map/ppermute | solution.py:193
  114.5 254.1 %all-gather.8.cloned.1.call-start = ((), (), s32[]{:S(2)}) async-start(), calls=%async_computation.8 | async-start | bytes 10485760 | tf_op jit(solution)/shard_map/all_gather | solution.py:190
  114.8 25.6 %collective-permute-start = (f32[256,1024]{0,1:T(8,128)}, f32[256,1024]{0,1:T(8,128)S(1)}, u32[]{:S(2)}, u32[]{:S(2)}) collective-permute-start(f32[256,1024]{0,1:T(8,128)} %bitcast.303), channel_id=1, source_target_pairs={{0,6},{2,4},{4,2},{6,0},{1,7},{3,5},{5,3},{7,1},{8,14},{10,12},{12... | collective-permute-start | bytes 3145736 | tf_op jit(solution)/shard_map/ppermute | solution.py:196
  130.5 112.7 %copy-start.19 = (f32[8,32,1,1,4,16]{1,5,0,2,4,3:T(8,128)}, f32[8,32,1,1,4,16]{1,5,0,2,4,3:T(8,128)S(1)}, u32[]{:S(2)}) copy-start(f32[8,32,1,1,4,16]{1,5,0,2,4,3:T(8,128)S(1)} %get-tuple-element.76) | copy-start | bytes 196612
  141.8 2.2 slice-start.1
  204.0 2.2 slice-start.2
  204.0 3.5 slice-start.3
  213.0 4.9 copy-start.6
  236.7 6.5 copy-start.12
  243.2 8.2 copy-start.2
  253.7 5.0 copy-start.11
  253.7 5.0 copy-start.20
  253.7 52.9 %all-to-all-start = ((f32[4,2,65,16,128]{4,3,2,1,0:T(8,128)}), f32[4,2,65,16,128]{4,3,2,1,0:T(8,128)}, u32[]{:S(2)}, u32[]{:S(2)}) async-start(f32[4,2,65,16,128]{4,3,2,1,0:T(8,128)} %copy.182), calls=%async_computation | async-start | bytes 8519680 | tf_op jit(solution)/shard_map/all_to_all | solution.py:289
  306.6 52.9 %all-to-all-start.2 = ((f32[4,2,65,16,128]{4,3,2,1,0:T(8,128)}), f32[4,2,65,16,128]{4,3,2,1,0:T(8,128)}, u32[]{:S(2)}, u32[]{:S(2)}) async-start(f32[4,2,65,16,128]{4,3,2,1,0:T(8,128)} %copy.193), calls=%async_computation.2 | async-start | bytes 8519680 | tf_op jit(solution)/shard_map/all_to_all | solution.py:289
  313.8 46.7 %copy-start.23 = (f32[256]{0:T(256)}, f32[256]{0:T(256)S(1)}, u32[]{:S(2)}) copy-start(f32[256]{0:T(256)S(1)} %compare_select_fusion.2) | copy-start | bytes 3076
  382.4 3.8 copy-start.5
  405.2 6.7 copy-start.10
  405.2 6.7 copy-start.21
  411.8 8.2 copy-start.3
  422.4 52.9 %all-to-all-start.1 = ((f32[4,2,65,16,128]{4,3,2,1,0:T(8,128)}), f32[4,2,65,16,128]{4,3,2,1,0:T(8,128)}, u32[]{:S(2)}, u32[]{:S(2)}) async-start(f32[4,2,65,16,128]{4,3,2,1,0:T(8,128)} %copy.188), calls=%async_computation.1 | async-start | bytes 8519680 | tf_op jit(solution)/shard_map/all_to_all | solution.py:289
  490.8 10.8 %copy-start.9 = (pred[8,65,32,128]{3,2,0,1:T(8,128)(4,1)S(1)}, pred[8,65,32,128]{3,2,0,1:T(8,128)(4,1)}, u32[]{:S(2)}) copy-start(pred[8,65,32,128]{3,2,0,1:T(8,128)(4,1)} %get-tuple-element.63) | copy-start | bytes 6389764
  490.8 10.8 %copy-start.22 = (f32[8,32,1,1,4,16]{1,5,0,2,4,3:T(8,128)S(1)}, f32[8,32,1,1,4,16]{1,5,0,2,4,3:T(8,128)}, u32[]{:S(2)}) copy-start(f32[8,32,1,1,4,16]{1,5,0,2,4,3:T(8,128)} %copy-done.19) | copy-start | bytes 196612
  500.2 116.1 %collective-permute-start.2 = (f32[256,16,512]{2,1,0:T(8,128)}, f32[256,16,512]{2,1,0:T(8,128)}, u32[]{:S(2)}, u32[]{:S(2)}) collective-permute-start(f32[256,16,512]{2,1,0:T(8,128)} %convolution_add_fusion.2.refs_0_), channel_id=1, source_target_pairs={{0,1},{1,0},{2,3},{3,2},{4,5},{5,4},{6,7},{7,6},{8,9},{9,8},{10,11... | collective-permute-start | bytes 25165832 | tf_op jit(solution)/shard_map/ppermute | solution.py:21
  568.5 2.0 copy-start.1
  579.1 6.4 copy-start.24
  585.5 8.0 copy-start.8
  611.2 94.6 %all-to-all-start.5 = ((f32[4,2,65,16,128]{4,3,2,1,0:T(8,128)}), f32[4,2,65,16,128]{4,3,2,1,0:T(8,128)}, u32[]{:S(2)}, u32[]{:S(2)}) async-start(f32[4,2,65,16,128]{4,3,2,1,0:T(8,128)} %copy.207), calls=%async_computation.5 | async-start | bytes 8519680 | tf_op jit(solution)/shard_map/all_to_all | solution.py:289
  623.3 51.2 %collective-permute-start.4 = (f32[256,1,512]{2,1,0:T(1,128)S(1)}, f32[256,1,512]{2,1,0:T(1,128)S(1)}, u32[]{:S(2)}, u32[]{:S(2)}) collective-permute-start(f32[256,1,512]{2,1,0:T(1,128)S(1)} %get-tuple-element.45), channel_id=1, source_target_pairs={{2,0},{4,2},{6,4},{8,6},{10,8},{12,10},{14,12},{16,14},{18,16},{20... | collective-permute-start | bytes 1572872 | tf_op jit(solution)/shard_map/ppermute | solution.py:308
  626.2 57.5 %collective-permute-start.3 = (f32[256,1,512]{2,1,0:T(1,128)S(1)}, f32[256,1,512]{2,1,0:T(1,128)S(1)}, u32[]{:S(2)}, u32[]{:S(2)}) collective-permute-start(f32[256,1,512]{2,1,0:T(1,128)S(1)} %get-tuple-element.46), channel_id=1, source_target_pairs={{0,2},{2,4},{4,6},{6,8},{8,10},{10,12},{12,14},{14,16},{16,18},{18... | collective-permute-start | bytes 1572872 | tf_op jit(solution)/shard_map/ppermute | solution.py:307
  674.5 9.2 copy-start.14
  721.4 11.3 %copy-start.7 = (pred[8,65,32,128]{3,2,0,1:T(8,128)(4,1)S(1)}, pred[8,65,32,128]{3,2,0,1:T(8,128)(4,1)}, u32[]{:S(2)}) copy-start(pred[8,65,32,128]{3,2,0,1:T(8,128)(4,1)} %get-tuple-element.65) | copy-start | bytes 6389764
  730.8 25.0 %collective-permute-start.5 = (f32[256,16,512]{2,1,0:T(8,128)}, f32[256,16,512]{2,1,0:T(8,128)}, u32[]{:S(2)}, u32[]{:S(2)}) collective-permute-start(f32[256,16,512]{2,1,0:T(8,128)} %convolution_add_fusion.1.refs_0_), channel_id=1, source_target_pairs={{0,1},{1,0},{2,3},{3,2},{4,5},{5,4},{6,7},{7,6},{8,9},{9,8},{10,11... | collective-permute-start | bytes 25165832 | tf_op jit(solution)/shard_map/ppermute | solution.py:21
  750.4 99.9 %all-to-all-start.3 = ((f32[4,2,65,16,128]{4,3,2,1,0:T(8,128)}), f32[4,2,65,16,128]{4,3,2,1,0:T(8,128)}, u32[]{:S(2)}, u32[]{:S(2)}) async-start(f32[4,2,65,16,128]{4,3,2,1,0:T(8,128)} %copy.199), calls=%async_computation.3 | async-start | bytes 8519680 | tf_op jit(solution)/shard_map/all_to_all | solution.py:289
  762.8 52.7 %collective-permute-start.7 = (f32[256,1,512]{2,1,0:T(1,128)S(1)}, f32[256,1,512]{2,1,0:T(1,128)S(1)}, u32[]{:S(2)}, u32[]{:S(2)}) collective-permute-start(f32[256,1,512]{2,1,0:T(1,128)S(1)} %get-tuple-element.43), channel_id=1, source_target_pairs={{2,0},{4,2},{6,4},{8,6},{10,8},{12,10},{14,12},{16,14},{18,16},{20... | collective-permute-start | bytes 1572872 | tf_op jit(solution)/shard_map/ppermute | solution.py:308
  766.2 58.1 %collective-permute-start.6 = (f32[256,1,512]{2,1,0:T(1,128)S(1)}, f32[256,1,512]{2,1,0:T(1,128)S(1)}, u32[]{:S(2)}, u32[]{:S(2)}) collective-permute-start(f32[256,1,512]{2,1,0:T(1,128)S(1)} %get-tuple-element.44), channel_id=1, source_target_pairs={{0,2},{2,4},{4,6},{6,8},{8,10},{10,12},{12,14},{14,16},{16,18},{18... | collective-permute-start | bytes 1572872 | tf_op jit(solution)/shard_map/ppermute | solution.py:307
  815.5 8.8 copy-start.13
  874.6 13.7 %copy-start = (f32[256,16,512]{2,1,0:T(8,128)}, f32[256,16,512]{2,1,0:T(8,128)S(1)}, u32[]{:S(2)}) copy-start(f32[256,16,512]{2,1,0:T(8,128)S(1)} %convolution_add_fusion.refs_0_) | copy-start | bytes 25165828
  874.6 13.6 %collective-permute-start.8 = (f32[256,16,512]{2,1,0:T(8,128)S(1)}, f32[256,16,512]{2,1,0:T(8,128)S(1)}, u32[]{:S(2)}, u32[]{:S(2)}) collective-permute-start(f32[256,16,512]{2,1,0:T(8,128)S(1)} %convolution_add_fusion.refs_0_), channel_id=1, source_target_pairs={{0,1},{1,0},{2,3},{3,2},{4,5},{5,4},{6,7},{7,6},{8,9},{9,8},{10,11... | collective-permute-start | bytes 25165832 | tf_op jit(solution)/shard_map/ppermute | solution.py:21
  888.3 3.7 copy-start.4
  892.0 17.0 %collective-permute-start.10 = (f32[256,1,512]{2,1,0:T(1,128)S(1)}, f32[256,1,512]{2,1,0:T(1,128)S(1)}, u32[]{:S(2)}, u32[]{:S(2)}) collective-permute-start(f32[256,1,512]{2,1,0:T(1,128)S(1)} %get-tuple-element.41), channel_id=1, source_target_pairs={{2,0},{4,2},{6,4},{8,6},{10,8},{12,10},{14,12},{16,14},{18,16},{20... | collective-permute-start | bytes 1572872 | tf_op jit(solution)/shard_map/ppermute | solution.py:308
  898.0 22.2 %collective-permute-start.9 = (f32[256,1,512]{2,1,0:T(1,128)S(1)}, f32[256,1,512]{2,1,0:T(1,128)S(1)}, u32[]{:S(2)}, u32[]{:S(2)}) collective-permute-start(f32[256,1,512]{2,1,0:T(1,128)S(1)} %get-tuple-element.42), channel_id=1, source_target_pairs={{0,2},{2,4},{4,6},{6,8},{8,10},{10,12},{12,14},{14,16},{16,18},{18... | collective-permute-start | bytes 1572872 | tf_op jit(solution)/shard_map/ppermute | solution.py:307
  909.0 11.2 %copy-start.17 = (f32[256,1,512]{2,1,0:T(1,128)}, f32[256,1,512]{2,1,0:T(1,128)S(1)}, u32[]{:S(2)}) copy-start(f32[256,1,512]{2,1,0:T(1,128)S(1)} %collective-permute-done.10.refs_3_) | copy-start | bytes 1572868
  (4 other events, 3.8 us)
Sparse Core Ops, SparseCore 0:
  26.7 87.7 all-gather.3
  116.1 87.8 all-gather.5
  205.5 147.7 all-gather.7

commit v3 on v2

--- a/solution.py
+++ b/solution.py
@@ -253,7 +253,6 @@
     backward = [((i + 1) % around, i) for i in range(around)]
     maps = {}
     sums = None
-    before = []
     for part in range(COL_PARTS):
         values = (jnp.concatenate(gathered[part], axis=0) * 0.5).astype(jnp.bfloat16)
         values = values.reshape(-1, TILE_ROWS, 2, 1, span)
@@ -284,11 +283,7 @@
             inside = radius <= jnp.repeat(limit, span)
             masked = jnp.where(inside[:, None], spectrum, 0.0)
             rows_done = jnp.einsum("rcqwl,rwcdsy->sdqyl", masked, row_table, precision=high)
-            if len(before) > 1:
-                rows_done, _ = lax.optimization_barrier((rows_done, before[-2]))
             arrived = lax.all_to_all(rows_done, "slab", split_axis=0, concat_axis=0, tiled=True)
-            if sums is not None:
-                arrived, sums = lax.optimization_barrier((arrived, sums))
             planes_done = jnp.einsum("sdqyl,sqdez->zyel", arrived, plane_table, precision=high)
             planes_done = planes_done.reshape(BOX, rows_here, 2 * CHUNK_BANDS * span)
             filtered = jnp.einsum("zyl,lx->zyx", planes_done, part_table, precision=high)
@@ -299,7 +294,6 @@
                 filtered = filtered + maps[start]
             maps[start] = filtered
             if part < COL_PARTS - 1:
-                before.append(filtered)
                 continue
             other = from_partner(filtered, "half", 0)
             head = (filtered[:, :1] - other[:, :1]) ** 2
@@ -309,7 +303,6 @@
             sums = blend(
                 filtered, other, low, high_rows, sums, CHUNK_BANDS, start + CHUNK_BANDS >= bands
             )
-            before.append(filtered)
     return sums[None]
 
 

time: 961 us -> 821 us (0.85)
  waiting for transfers between devices: 388 us -> 278 us
  blocking collectives: 51.2 us -> 0 us
  starting transfers between devices: 47.6 us -> 74.6 us
  matrix products: 220 us -> 207 us
    ppermute x3, waiting for transfers between devices: 109 us -> 0.01 us  [on_device(): high_rows = lax.ppermute(head, ('particle', 'slab'), backward)]
    all_gather x3, waiting for transfers between devices: 120 us -> 183 us  [gather(): return lax.all_gather(array, 'particle', axis=0, tiled=True)]
    all_to_all x1 -> x0, blocking collectives: 51.2 us -> none  [on_device(): lax.all_to_all(rows_done, 'slab', split_axis=0, concat_axis=0, tiled=True)]
    ppermute x3, waiting for transfers between devices: 29.2 us -> 0.01 us  [on_device(): low = lax.ppermute(tail, ('particle', 'slab'), forward)]
    all_to_all x5 -> x6, waiting for transfers between devices: 82.4 us -> 58.5 us  [on_device(): lax.all_to_all(rows_done, 'slab', split_axis=0, concat_axis=0, tiled=True)]
    ppermute x3, starting transfers between devices: 12.4 us -> 36.1 us  [on_device(): high_rows = lax.ppermute(head, ('particle', 'slab'), backward)]
    dot_general x6, matrix products: 51.6 us -> 34.4 us  [on_device(): jnp.einsum('zyl,lx->zyx', planes_done, part_table, precision=high)]
    ppermute x3, waiting for transfers between devices: 12.8 us -> 0.01 us  [from_partner(): lax.ppermute(array, axis, [(i, i ^ 1 << bit) for i in range(lax.axis_size...]
  transfers between devices with their start and end apart: 19 -> 20, of which waited for: 14 -> 8; matrix products, arithmetic and copies ran while one was open for 23% -> 42% of each run, Pallas kernels for 5% -> 6%
where the time goes in v3:
time: 821 us; the launch traced here: 811 us
  waiting for transfers between devices  278 us (34%)
  matrix products  207 us (25%)
  local copies, waits for them, and re-layouts  106 us (13%)
  starting transfers between devices  74.6 us (9%)
  Pallas kernels  70.9 us (9%)
  other arithmetic  61.8 us (8%)
  between operations  14.2 us (2%)
    all_gather x3, waiting for transfers between devices, gather(): return lax.all_gather(array, 'particle', axis=0, tiled=True)  183 us
    pallas_call x3, Pallas kernels, blend(): pl.pallas_call(functools.partial(blend_kernel, first, last, step_planes),...  70.9 us
    dot_general x6, matrix products, on_device(): jnp.einsum('rcqwl,rwcdsy->sdqyl', masked, row_table, precision=high)  70.7 us
    all_to_all x6, waiting for transfers between devices, on_device(): lax.all_to_all(rows_done, 'slab', split_axis=0, concat_axis=0, tiled=True)  58.5 us
    dot_general x6, matrix products, on_device(): jnp.einsum('sdqyl,sqdez->zyel', arrived, plane_table, precision=high)  51.5 us
    dot_general x2, matrix products, on_device(): jnp.einsum('te,erck->rctk', place_other, values[:, 1:], preferred_element...  42 us
    ppermute x3, starting transfers between devices, on_device(): high_rows = lax.ppermute(head, ('particle', 'slab'), backward)  36.1 us
    dot_general x6, matrix products, on_device(): jnp.einsum('zyl,lx->zyx', planes_done, part_table, precision=high)  34.4 us
  transfers between devices with their start and end apart: 20, of which 8 were waited for; matrix products, arithmetic and copies ran while one was open for 42% of the time, Pallas kernels for 6%

profile of v3, /device:TPU:25, one launch (start us, length us, event | category | flops | bytes accessed | tf_op | source)
XLA Modules:
  0.0 811.2 jit_solution(399133031256697182)
XLA Ops:
  29.9 25.7 %collective-permute-done.1 = f32[256,1152]{0,1:T(8,128)} collective-permute-done((f32[256,1152]{0,1:T(8,128)S(1)}, f32[256,1152]{0,1:T(8,128)}, u32[]{:S(2)}, u32[]{:S(2)}) %collective-permute-start.1) | collective-permute-done | bytes 1179680 | tf_op jit(solution)/shard_map/ppermute | solution.py:193
  55.5 60.0 %all-gather.4.cloned.1.call-done = f32[1024,1152]{0,1:T(8,128)} async-done(((f32[256,1152]{0,1:T(8,128)}), f32[1024,1152]{0,1:T(8,128)}) %all-gather.4.cloned.1.call-update) | async-done | bytes 4718608 | tf_op jit(solution)/shard_map/all_gather | solution.py:190
  119.9 10.8 %fusion.53 = (pred[8,65,32,128]{3,2,0,1:T(8,128)(4,1)}, pred[8,65,32,128]{3,2,0,1:T(8,128)(4,1)}, pred[8,65,32,128]{3,2,0,1:T(8,128)(4,1)}, pred[8,65,32,128]{3,...) fusion(s32[128]{0:T(128)S(1)} %le.80, s32[128]{0:T(128)S(1)} %integer_pow.57, ...), kind=kLoop, calls=%fused_computation.59 | loop fusion | flops 21299200 | bytes 12865280 | tf_op jit(solution)/shard_map/le | solution.py:283
  131.7 9.9 %collective-permute-done = f32[256,1024]{0,1:T(8,128)S(1)} collective-permute-done((f32[256,1024]{0,1:T(8,128)}, f32[256,1024]{0,1:T(8,128)S(1)}, u32[]{:S(2)}, u32[]{:S(2)}) %collective-permute-start) | collective-permute-done | bytes 1048608 | tf_op jit(solution)/shard_map/ppermute | solution.py:196
  143.1 61.8 %all-gather.6.cloned.1.call-done = f32[1024,1152]{0,1:T(8,128)} async-done(((f32[256,1152]{0,1:T(8,128)}), f32[1024,1152]{0,1:T(8,128)}) %all-gather.6.cloned.1.call-update) | async-done | bytes 4718608 | tf_op jit(solution)/shard_map/all_gather | solution.py:190
  223.0 18.9 %convolution_bitcast_fusion = f32[7,2,2080,128]{3,2,1,0:T(8,128)} fusion(s32[2048]{0:T(1024)S(1)} %get-tuple-element.58, bf16[2048]{0:T(1024)(128)(2,1)S(1)} %pad_maximum_fusion.7, bf16[2048,8,2,128]{0,3,2,1:T(8,128)(2,1)S(1)} %bitcast.303), kind=kOutput, calls=%fused_computation.30 | convolution fusion | flops 15275786240 | bytes 22261760 | tf_op jit(solution)/shard_map/te,erck->rctk/dot_general | solution.py:264
  241.9 6.4 pad_maximum_fusion.1
  248.3 8.2 %fusion.105 = f32[4,2,65,16,128]{4,3,2,0,1:T(8,128)S(1)} fusion(f32[8,2,65,32,128]{4,3,2,1,0:T(8,128)S(1)} %bitcast.280, pred[8,65,32,128]{3,2,0,1:T(8,128)(4,1)S(1)} %copy-done.13, f32[8,32,1,1,4,16]{1,5,0,2,4,3:T(8,128)S(1)} %get-tuple-element.56, f32[8,32,1,1,4,16]{1,5,0,2,4,3:T(8,128)S(1)} %get-tuple-element.55, ...), kind=kOutput, calls=%fused_computation.102 | convolution fusion | flops 3276013568 | bytes 23625728 | tf_op jit(solution)/shard_map/rcqwl,rwcdsy->sdqyl/dot_general | solution.py:285
  258.8 5.3 all-to-all-start.5
  264.2 15.9 %fusion.93 = f32[4,2,65,16,128]{4,3,2,0,1:T(8,128)S(1)} fusion(f32[8,2,65,32,128]{4,3,2,1,0:T(8,128)} %bitcast.281, pred[8,65,32,128]{3,2,0,1:T(8,128)(4,1)S(1)} %copy-done.12, f32[8,32,1,1,4,16]{1,5,0,2,4,3:T(8,128)S(1)} %get-tuple-element.56, f32[8,32,1,1,4,16]{1,5,0,2,4,3:T(8,128)S(1)} %get-tuple-element.55, ...), kind=kOutput, calls=%fused_computation.98 | convolution fusion | flops 3276013568 | bytes 23625728 | tf_op jit(solution)/shard_map/rcqwl,rwcdsy->sdqyl/dot_general | solution.py:285
  282.5 7.9 fusion.99
  292.8 61.6 %all-gather.8.cloned.1.call-done = f32[1024,2048]{0,1:T(8,128)} async-done(((f32[256,2048]{0,1:T(8,128)}), f32[1024,2048]{0,1:T(8,128)}) %all-gather.8.cloned.1.call-update) | async-done | bytes 8388624 | tf_op jit(solution)/shard_map/all_gather | solution.py:190
  366.6 6.9 broadcast_in_dim.236
  373.4 23.1 %convolution_bitcast_fusion.1 = f32[7,2,2080,128]{3,2,1,0:T(8,128)} fusion(s32[2048]{0:T(1024)S(1)} %get-tuple-element.58, bf16[2048]{0:T(1024)(128)(2,1)S(1)} %pad_maximum_fusion.7, bf16[2048,8,2,128]{0,3,2,1:T(8,128)(2,1)} %bitcast.300), kind=kOutput, calls=%fused_computation.31 | convolution fusion | flops 15275786240 | bytes 22261760 | tf_op jit(solution)/shard_map/te,erck->rctk/dot_general | solution.py:264
  396.5 17.8 %all-to-all-done.1 = f32[4,2,65,16,128]{4,3,2,1,0:T(8,128)} async-done(((f32[4,2,65,16,128]{4,3,2,1,0:T(8,128)}), f32[4,2,65,16,128]{4,3,2,1,0:T(8,128)}, u32[]{:S(2)}, u32[]{:S(2)}) %all-to-all-start.1) | async-done | bytes 4259872 | tf_op jit(solution)/shard_map/all_to_all | solution.py:286
  414.3 5.0 all-to-all-start.3
  423.0 6.2 pad_maximum_fusion
  429.2 8.2 %fusion.102 = f32[4,2,65,16,128]{4,3,2,0,1:T(8,128)S(1)} fusion(f32[8,2,65,32,128]{4,3,2,1,0:T(8,128)S(1)} %bitcast.277, pred[8,65,32,128]{3,2,0,1:T(8,128)(4,1)S(1)} %copy-done.10, f32[8,32,1,1,4,16]{1,5,0,2,4,3:T(8,128)S(1)} %get-tuple-element.56, f32[8,32,1,1,4,16]{1,5,0,2,4,3:T(8,128)S(1)} %get-tuple-element.55, ...), kind=kOutput, calls=%fused_computation.101 | convolution fusion | flops 3276013568 | bytes 23625728 | tf_op jit(solution)/shard_map/rcqwl,rwcdsy->sdqyl/dot_general | solution.py:285
  439.8 27.1 %all-to-all-done.3 = f32[4,2,65,16,128]{4,3,2,1,0:T(8,128)} async-done(((f32[4,2,65,16,128]{4,3,2,1,0:T(8,128)}), f32[4,2,65,16,128]{4,3,2,1,0:T(8,128)}, u32[]{:S(2)}, u32[]{:S(2)}) %all-to-all-start.3) | async-done | bytes 4259872 | tf_op jit(solution)/shard_map/all_to_all | solution.py:286
  466.9 5.1 all-to-all-start.4
  475.4 13.1 %fusion.123 = f32[256,16,2,128]{0,3,1,2:T(8,128)} fusion(f32[4,2,65,16,128]{4,3,2,1,0:T(8,128)} %all-to-all-done.5, f32[4,65,1,2,256]{4,1,0,2,3:T(8,128)S(1)} %get-tuple-element.38, f32[4,65,1,2,256]{4,1,0,2,3:T(8,128)S(1)} %get-tuple-element.37), kind=kOutput, calls=%fused_computation.108 | convolution fusion | flops 3271823360 | bytes 9519104 | tf_op jit(solution)/shard_map/sdqyl,sqdez->zyel/dot_general | solution.py:287
  488.5 15.2 %fusion.96 = f32[4,2,65,16,128]{4,3,2,0,1:T(8,128)S(1)} fusion(f32[8,2,65,32,128]{4,3,2,1,0:T(8,128)} %bitcast.278, pred[8,65,32,128]{3,2,0,1:T(8,128)(4,1)S(1)} %copy-done.9, f32[8,32,1,1,4,16]{1,5,0,2,4,3:T(8,128)S(1)} %get-tuple-element.56, f32[8,32,1,1,4,16]{1,5,0,2,4,3:T(8,128)S(1)} %get-tuple-element.55, ...), kind=kOutput, calls=%fused_computation.99 | convolution fusion | flops 3276013568 | bytes 23625728 | tf_op jit(solution)/shard_map/rcqwl,rwcdsy->sdqyl/dot_general | solution.py:285
  506.1 13.5 %all-to-all-done.4 = f32[4,2,65,16,128]{4,3,2,1,0:T(8,128)} async-done(((f32[4,2,65,16,128]{4,3,2,1,0:T(8,128)}), f32[4,2,65,16,128]{4,3,2,1,0:T(8,128)}, u32[]{:S(2)}, u32[]{:S(2)}) %all-to-all-start.4) | async-done | bytes 4259872 | tf_op jit(solution)/shard_map/all_to_all | solution.py:286
  519.6 5.3 all-to-all-start.2
  530.1 5.5 copy.245
  537.0 7.7 fusion.117
  547.1 5.5 copy.235
  552.5 7.7 fusion.111
  562.6 5.5 copy.225
  568.1 15.3 %fusion.90 = f32[4,2,65,16,128]{4,3,2,0,1:T(8,128)S(1)} fusion(f32[8,2,65,32,128]{4,3,2,1,0:T(8,128)} %bitcast.279, pred[8,65,32,128]{3,2,0,1:T(8,128)(4,1)} %get-tuple-element.44, f32[8,32,1,1,4,16]{1,5,0,2,4,3:T(8,128)S(1)} %get-tuple-element.56, f32[8,32,1,1,4,16]{1,5,0,2,4,3:T(8,128)S(1)} %get-tuple-element.55, ...), kind=kOutput, calls=%fused_computation.97 | convolution fusion | flops 3276013568 | bytes 23625728 | tf_op jit(solution)/shard_map/rcqwl,rwcdsy->sdqyl/dot_general | solution.py:285
  585.8 5.0 all-to-all-start
  590.9 7.7 fusion.120
  600.9 5.5 copy.240
  606.4 5.6 fusion.219
  612.0 6.4 add_add_fusion.refs_0_
  619.9 7.7 fusion.114
  629.9 5.5 copy.230
  635.4 5.8 fusion.218
  641.2 6.5 add_add_fusion.1.refs_0_
  647.8 7.7 fusion.108
  657.8 5.5 copy.220
  663.3 5.8 fusion.217
  674.0 9.3 %fusion.131 = (f32[256,1,512]{2,1,0:T(1,128)S(1)}, f32[256,1,512]{2,1,0:T(1,128)S(1)}) fusion(f32[256,16,512]{2,1,0:T(8,128)} %collective-permute-done.8.refs_1_, f32[256,16,512]{2,1,0:T(8,128)} %add_add_fusion.refs_0_), kind=kLoop, calls=%fused_computation.130 | loop fusion | flops 524288 | bytes 3145728 | tf_op jit(solution)/shard_map/integer_pow | solution.py:299
  686.9 7.7 fusion.133
  701.7 30.0 %collective-permute-start.4 = (f32[256,1,512]{2,1,0:T(1,128)S(1)}, f32[256,1,512]{2,1,0:T(1,128)}, u32[]{:S(2)}, u32[]{:S(2)}) collective-permute-start(f32[256,1,512]{2,1,0:T(1,128)S(1)} %get-tuple-element.25), channel_id=1, source_target_pairs={{2,0},{4,2},{6,4},{8,6},{10,8},{12,10},{14,12},{16,14},{18,16},{20... | collective-permute-start | bytes 1572872 | tf_op jit(solution)/shard_map/ppermute | solution.py:302
  732.5 21.4 %shard_map.64 = (f32[256,16,256]{2,1,0:T(8,128)}, f32[256,16,256]{2,1,0:T(8,128)}) custom-call(f32[256,16,512]{2,1,0:T(8,128)} %add_add_fusion.refs_0_, f32[256,16,512]{2,1,0:T(8,128)} %collective-permute-done.8.refs_1_, f32[256,1,512]{2,1,0:T(1,128)} %copy-done.18, f32[256,1,512]{2,1,0:T(1,128)} %copy-done.16), custom_call_target="tpu_custom_call" | custom-call | flops 41943040 | bytes 33554432 | tf_op jit(solution)/shard_map/pallas_call | solution.py:119
  754.9 25.0 %shard_map.65 = (f32[256,16,256]{2,1,0:T(8,128)}, f32[256,16,256]{2,1,0:T(8,128)}) custom-call(f32[256,16,512]{2,1,0:T(8,128)} %add_add_fusion.1.refs_0_, f32[256,16,512]{2,1,0:T(8,128)} %collective-permute-done.5.refs_1_, f32[256,1,512]{2,1,0:T(1,128)} %copy-done.15, f32[256,1,512]{2,1,0:T(1,128)} %copy-done.17, f32[256,16,256]{2,1,0:T(8,128)} %get-tuple-element.17.refs_4_, ...), custom_call_target="tpu_custom_call" | custom-call | flops 41943040 | bytes 33554432 | tf_op jit(solution)/shard_map/pallas_call | solution.py:119
  779.9 24.5 %shard_map.66 = f32[256,16,256]{2,1,0:T(8,128)} custom-call(f32[256,16,512]{2,1,0:T(8,128)} %copy-done, f32[256,16,512]{2,1,0:T(8,128)} %copy-done.6, f32[256,1,512]{2,1,0:T(1,128)} %collective-permute-done.3.refs_2_, f32[256,1,512]{2,1,0:T(1,128)} %collective-permute-done.4.refs_3_, f32[256,16,256]{2,1,0:T(8,128)} %get-tuple-element.19.refs_4_, ...), custom_call_target="tpu_custom_call" | custom-call | flops 41943040 | bytes 33554432 | tf_op jit(solution)/shard_map/pallas_call | solution.py:119
  (223 shorter events, 118.4 us)
Async XLA Ops:
  6.5 8.6 %copy-start.28 = (f32[2]{0:T(128)S(1)}, f32[2]{0:T(128)}, u32[]{:S(2)}) copy-start(f32[2]{0:T(128)} %constant.163.clone) | copy-start | bytes 28
  6.5 109.0 %all-gather.4.cloned.1.call-start = ((), (), s32[]{:S(2)}) async-start(), calls=%async_computation.6 | async-start | bytes 5898240 | tf_op jit(solution)/shard_map/all_gather | solution.py:190
  19.9 4.7 copy-start.25
  19.9 4.7 copy-start.26
  19.9 5.0 slice-start.11
  26.1 92.7 %copy-start.27 = (s32[6]{0:T(128)S(1)}, s32[6]{0:T(128)}, u32[]{:S(2)}) copy-start(s32[6]{0:T(128)} %param.10) | copy-start | bytes 76
  27.6 177.4 %all-gather.6.cloned.1.call-start = ((), (), s32[]{:S(2)}) async-start(), calls=%async_computation.7 | async-start | bytes 5898240 | tf_op jit(solution)/shard_map/all_gather | solution.py:190
  27.6 27.9 %collective-permute-start.1 = (f32[256,1152]{0,1:T(8,128)S(1)}, f32[256,1152]{0,1:T(8,128)}, u32[]{:S(2)}, u32[]{:S(2)}) collective-permute-start(f32[256,1152]{0,1:T(8,128)S(1)} %get-tuple-element.53), channel_id=1, source_target_pairs={{0,6},{2,4},{4,2},{6,0},{1,7},{3,5},{5,3},{7,1},{8,14},{10,12},{12... | collective-permute-start | bytes 3538952 | tf_op jit(solution)/shard_map/ppermute | solution.py:193
  115.5 238.8 %all-gather.8.cloned.1.call-start = ((), (), s32[]{:S(2)}) async-start(), calls=%async_computation.8 | async-start | bytes 10485760 | tf_op jit(solution)/shard_map/all_gather | solution.py:190
  116.1 25.6 %collective-permute-start = (f32[256,1024]{0,1:T(8,128)}, f32[256,1024]{0,1:T(8,128)S(1)}, u32[]{:S(2)}, u32[]{:S(2)}) collective-permute-start(f32[256,1024]{0,1:T(8,128)} %bitcast.307), channel_id=1, source_target_pairs={{0,6},{2,4},{4,2},{6,0},{1,7},{3,5},{5,3},{7,1},{8,14},{10,12},{12... | collective-permute-start | bytes 3145736 | tf_op jit(solution)/shard_map/ppermute | solution.py:196
  205.0 3.9 slice-start.8
  210.3 8.4 %copy-start.21 = (s32[2048]{0:T(1024)}, s32[2048]{0:T(1024)S(1)}, u32[]{:S(2)}) copy-start(s32[2048]{0:T(1024)S(1)} %get-tuple-element.57) | copy-start | bytes 24580
  218.6 4.4 copy-start.7
  241.9 6.5 copy-start.13
  248.3 8.2 %copy-start.2 = (f32[8,2,2080,128]{3,2,1,0:T(8,128)}, f32[8,2,2080,128]{3,2,1,0:T(8,128)S(1)}, u32[]{:S(2)}) copy-start(f32[8,2,2080,128]{3,2,1,0:T(8,128)S(1)} %pad_maximum_fusion.1) | copy-start | bytes 51118084
  258.8 5.3 copy-start.12
  258.8 23.7 %slice-start = ((s8[17039360]{0:T(1024)(128)(4,1)}), s8[262144]{0:T(1024)(128)(4,1)S(1)}, s32[]{:S(2)}) async-start(s8[17039360]{0:T(1024)(128)(4,1)} %bitcast.282), calls=%async_computation.9 | async-start | bytes 524288
  258.8 102.8 %all-to-all-start.5 = ((f32[4,2,65,16,128]{4,3,2,1,0:T(8,128)}), f32[4,2,65,16,128]{4,3,2,1,0:T(8,128)}, u32[]{:S(2)}, u32[]{:S(2)}) async-start(f32[4,2,65,16,128]{4,3,2,1,0:T(8,128)} %copy.206), calls=%async_computation.5 | async-start | bytes 8519680 | tf_op jit(solution)/shard_map/all_to_all | solution.py:286
  264.1 18.4 %slice-start.1 = ((s8[17039360]{0:T(1024)(128)(4,1)}), s8[4194304]{0:T(1024)(128)(4,1)S(1)}, s32[]{:S(2)}) async-start(s8[17039360]{0:T(1024)(128)(4,1)} %bitcast.282), calls=%async_computation.10 | async-start | bytes 8388608
  264.1 18.4 %slice-start.2 = ((s8[17039360]{0:T(1024)(128)(4,1)}), s8[4194304]{0:T(1024)(128)(4,1)S(1)}, s32[]{:S(2)}) async-start(s8[17039360]{0:T(1024)(128)(4,1)} %bitcast.282), calls=%async_computation.11 | async-start | bytes 8388608
  264.1 18.4 %slice-start.3 = ((s8[17039360]{0:T(1024)(128)(4,1)}), s8[4194304]{0:T(1024)(128)(4,1)S(1)}, s32[]{:S(2)}) async-start(s8[17039360]{0:T(1024)(128)(4,1)} %bitcast.282), calls=%async_computation.12 | async-start | bytes 8388608
  264.2 18.3 %slice-start.4 = ((s8[17039360]{0:T(1024)(128)(4,1)}), s8[4194304]{0:T(1024)(128)(4,1)S(1)}, s32[]{:S(2)}) async-start(s8[17039360]{0:T(1024)(128)(4,1)} %bitcast.282), calls=%async_computation.13 | async-start | bytes 8388608
  361.6 52.7 %all-to-all-start.1 = ((f32[4,2,65,16,128]{4,3,2,1,0:T(8,128)}), f32[4,2,65,16,128]{4,3,2,1,0:T(8,128)}, u32[]{:S(2)}, u32[]{:S(2)}) async-start(f32[4,2,65,16,128]{4,3,2,1,0:T(8,128)} %copy.182), calls=%async_computation.1 | async-start | bytes 8519680 | tf_op jit(solution)/shard_map/all_to_all | solution.py:286
  396.5 22.8 %copy-start.22 = (s32[2048]{0:T(1024)S(1)}, s32[2048]{0:T(1024)}, u32[]{:S(2)}) copy-start(s32[2048]{0:T(1024)} %copy-done.21) | copy-start | bytes 24580
  414.3 52.6 %all-to-all-start.3 = ((f32[4,2,65,16,128]{4,3,2,1,0:T(8,128)}), f32[4,2,65,16,128]{4,3,2,1,0:T(8,128)}, u32[]{:S(2)}, u32[]{:S(2)}) async-start(f32[4,2,65,16,128]{4,3,2,1,0:T(8,128)} %copy.194), calls=%async_computation.3 | async-start | bytes 8519680 | tf_op jit(solution)/shard_map/all_to_all | solution.py:286
  423.0 6.2 copy-start.10
  429.2 8.2 %copy-start.1 = (f32[8,2,2080,128]{3,2,1,0:T(8,128)}, f32[8,2,2080,128]{3,2,1,0:T(8,128)S(1)}, u32[]{:S(2)}) copy-start(f32[8,2,2080,128]{3,2,1,0:T(8,128)S(1)} %pad_maximum_fusion) | copy-start | bytes 51118084
  439.8 32.2 %copy-start.19 = (f32[64,2,256]{2,0,1:T(8,128)S(1)}, f32[64,2,256]{2,0,1:T(8,128)}, u32[]{:S(2)}) copy-start(f32[64,2,256]{2,0,1:T(8,128)} %get-tuple-element.48) | copy-start | bytes 393220
  439.8 32.3 %copy-start.20 = (f32[64,2,256]{2,0,1:T(8,128)S(1)}, f32[64,2,256]{2,0,1:T(8,128)}, u32[]{:S(2)}) copy-start(f32[64,2,256]{2,0,1:T(8,128)} %get-tuple-element.49) | copy-start | bytes 393220
  439.8 32.3 %copy-start.24 = (f32[2,2]{1,0:T(2,128)S(1)}, f32[2,2]{1,0:T(2,128)}, u32[]{:S(2)}) copy-start(f32[2,2]{1,0:T(2,128)} %compare_convert_fusion) | copy-start | bytes 52
  466.9 52.7 %all-to-all-start.4 = ((f32[4,2,65,16,128]{4,3,2,1,0:T(8,128)}), f32[4,2,65,16,128]{4,3,2,1,0:T(8,128)}, u32[]{:S(2)}, u32[]{:S(2)}) async-start(f32[4,2,65,16,128]{4,3,2,1,0:T(8,128)} %copy.201), calls=%async_computation.4 | async-start | bytes 8519680 | tf_op jit(solution)/shard_map/all_to_all | solution.py:286
  475.4 13.1 %copy-start.9 = (pred[8,65,32,128]{3,2,0,1:T(8,128)(4,1)S(1)}, pred[8,65,32,128]{3,2,0,1:T(8,128)(4,1)}, u32[]{:S(2)}) copy-start(pred[8,65,32,128]{3,2,0,1:T(8,128)(4,1)} %get-tuple-element.43) | copy-start | bytes 6389764
  519.6 66.2 %all-to-all-start.2 = ((f32[4,2,65,16,128]{4,3,2,1,0:T(8,128)}), f32[4,2,65,16,128]{4,3,2,1,0:T(8,128)}, u32[]{:S(2)}, u32[]{:S(2)}) async-start(f32[4,2,65,16,128]{4,3,2,1,0:T(8,128)} %copy.189), calls=%async_computation.2 | async-start | bytes 8519680 | tf_op jit(solution)/shard_map/all_to_all | solution.py:286
  585.8 61.9 %all-to-all-start = ((f32[4,2,65,16,128]{4,3,2,1,0:T(8,128)}), f32[4,2,65,16,128]{4,3,2,1,0:T(8,128)}, u32[]{:S(2)}, u32[]{:S(2)}) async-start(f32[4,2,65,16,128]{4,3,2,1,0:T(8,128)} %copy.174), calls=%async_computation | async-start | bytes 8519680 | tf_op jit(solution)/shard_map/all_to_all | solution.py:286
  606.4 5.6 copy-start.4
  618.5 55.6 %collective-permute-start.8 = (f32[256,16,512]{2,1,0:T(8,128)}, f32[256,16,512]{2,1,0:T(8,128)}, u32[]{:S(2)}, u32[]{:S(2)}) collective-permute-start(f32[256,16,512]{2,1,0:T(8,128)} %add_add_fusion.refs_0_), channel_id=1, source_target_pairs={{0,1},{1,0},{2,3},{3,2},{4,5},{5,4},{6,7},{7,6},{8,9},{9,8},{10,11... | collective-permute-start | bytes 25165832 | tf_op jit(solution)/shard_map/ppermute | solution.py:21
  635.4 5.8 copy-start.5
  647.8 39.2 %collective-permute-start.5 = (f32[256,16,512]{2,1,0:T(8,128)}, f32[256,16,512]{2,1,0:T(8,128)}, u32[]{:S(2)}, u32[]{:S(2)}) collective-permute-start(f32[256,16,512]{2,1,0:T(8,128)} %add_add_fusion.1.refs_0_), channel_id=1, source_target_pairs={{0,1},{1,0},{2,3},{3,2},{4,5},{5,4},{6,7},{7,6},{8,9},{9,8},{10,11... | collective-permute-start | bytes 25165832 | tf_op jit(solution)/shard_map/ppermute | solution.py:21
  663.3 5.8 copy-start.3
  673.5 26.7 %copy-start = (f32[256,16,512]{2,1,0:T(8,128)}, f32[256,16,512]{2,1,0:T(8,128)S(1)}, u32[]{:S(2)}) copy-start(f32[256,16,512]{2,1,0:T(8,128)S(1)} %add_add_fusion.2.refs_0_) | copy-start | bytes 25165828
  673.5 24.4 %collective-permute-start.2 = (f32[256,16,512]{2,1,0:T(8,128)S(1)}, f32[256,16,512]{2,1,0:T(8,128)S(1)}, u32[]{:S(2)}, u32[]{:S(2)}) collective-permute-start(f32[256,16,512]{2,1,0:T(8,128)S(1)} %add_add_fusion.2.refs_0_), channel_id=1, source_target_pairs={{0,1},{1,0},{2,3},{3,2},{4,5},{5,4},{6,7},{7,6},{8,9},{9,8},{10,11... | collective-permute-start | bytes 25165832 | tf_op jit(solution)/shard_map/ppermute | solution.py:21
  683.4 18.3 %collective-permute-start.10 = (f32[256,1,512]{2,1,0:T(1,128)S(1)}, f32[256,1,512]{2,1,0:T(1,128)S(1)}, u32[]{:S(2)}, u32[]{:S(2)}) collective-permute-start(f32[256,1,512]{2,1,0:T(1,128)S(1)} %get-tuple-element.21), channel_id=1, source_target_pairs={{2,0},{4,2},{6,4},{8,6},{10,8},{12,10},{14,12},{16,14},{18,16},{20... | collective-permute-start | bytes 1572872 | tf_op jit(solution)/shard_map/ppermute | solution.py:302
  686.9 44.7 %collective-permute-start.9 = (f32[256,1,512]{2,1,0:T(1,128)S(1)}, f32[256,1,512]{2,1,0:T(1,128)S(1)}, u32[]{:S(2)}, u32[]{:S(2)}) collective-permute-start(f32[256,1,512]{2,1,0:T(1,128)S(1)} %get-tuple-element.22), channel_id=1, source_target_pairs={{0,2},{2,4},{4,6},{6,8},{8,10},{10,12},{12,14},{14,16},{16,18},{18... | collective-permute-start | bytes 1572872 | tf_op jit(solution)/shard_map/ppermute | solution.py:301
  694.6 59.2 %collective-permute-start.6 = (f32[256,1,512]{2,1,0:T(1,128)}, f32[256,1,512]{2,1,0:T(1,128)S(1)}, u32[]{:S(2)}, u32[]{:S(2)}) collective-permute-start(f32[256,1,512]{2,1,0:T(1,128)} %get-tuple-element.24), channel_id=1, source_target_pairs={{0,2},{2,4},{4,6},{6,8},{8,10},{10,12},{12,14},{14,16},{16,18},{18... | collective-permute-start | bytes 1572872 | tf_op jit(solution)/shard_map/ppermute | solution.py:301
  695.2 58.6 %collective-permute-start.7 = (f32[256,1,512]{2,1,0:T(1,128)S(1)}, f32[256,1,512]{2,1,0:T(1,128)S(1)}, u32[]{:S(2)}, u32[]{:S(2)}) collective-permute-start(f32[256,1,512]{2,1,0:T(1,128)S(1)} %get-tuple-element.23), channel_id=1, source_target_pairs={{2,0},{4,2},{6,4},{8,6},{10,8},{12,10},{14,12},{16,14},{18,16},{20... | collective-permute-start | bytes 1572872 | tf_op jit(solution)/shard_map/ppermute | solution.py:302
  701.7 78.2 %collective-permute-start.3 = (f32[256,1,512]{2,1,0:T(1,128)S(1)}, f32[256,1,512]{2,1,0:T(1,128)}, u32[]{:S(2)}, u32[]{:S(2)}) collective-permute-start(f32[256,1,512]{2,1,0:T(1,128)S(1)} %get-tuple-element.26), channel_id=1, source_target_pairs={{0,2},{2,4},{4,6},{6,8},{8,10},{10,12},{12,14},{14,16},{16,18},{18... | collective-permute-start | bytes 1572872 | tf_op jit(solution)/shard_map/ppermute | solution.py:301
  701.7 30.0 %copy-start.16 = (f32[256,1,512]{2,1,0:T(1,128)}, f32[256,1,512]{2,1,0:T(1,128)S(1)}, u32[]{:S(2)}) copy-start(f32[256,1,512]{2,1,0:T(1,128)S(1)} %collective-permute-done.10.refs_3_) | copy-start | bytes 1572868
  701.7 78.2 %collective-permute-start.4 = (f32[256,1,512]{2,1,0:T(1,128)S(1)}, f32[256,1,512]{2,1,0:T(1,128)}, u32[]{:S(2)}, u32[]{:S(2)}) collective-permute-start(f32[256,1,512]{2,1,0:T(1,128)S(1)} %get-tuple-element.25), channel_id=1, source_target_pairs={{2,0},{4,2},{6,4},{8,6},{10,8},{12,10},{14,12},{16,14},{18,16},{20... | collective-permute-start | bytes 1572872 | tf_op jit(solution)/shard_map/ppermute | solution.py:302
  (13 other events, 27.1 us)
Sparse Core Ops, SparseCore 0:
  27.7 87.7 all-gather.3
  117.1 87.8 all-gather.5
  206.5 147.7 all-gather.7
